TPU v7x, 256 devices: a whole 4x4x8 slice. The times are simulated.
256 devices in a mesh: dp: 4 (over y_lo, core), tensor: 64 (over y_hi, x, z).
Axes of the slice: x: 4, y: 4 (y_hi: 2, y_lo: 2; y = y_hi * 2 + y_lo), z: 8, core: 2. Of those that a mesh axis runs over, the one named last changes fastest.
Arguments:
- hidden: bfloat16 [1024, 5120], P('dp'), may hold values from -12 to 12, as said below
- head_weight: bfloat16 [5120, 81920], P('dp', 'tensor'), as said below
- prompt_ids: int32 [64, 32], P('dp'), may hold values from 0 to 81919, as said below
- prompt_counts: int32 [64, 32], P('dp'), may hold values from 1 to 8
- sampled_ids: int32 [64, 16], P('dp'), may hold values from 0 to 81919, as said below
- token_mask: int32 [64, 16], P('dp'), may hold values 0 or 1
- rewards: float32 [64], P('dp'), may hold values from -4 to 4
Outputs:
- logprobs: float32 [64, 16], P('dp')
- grad_hidden: bfloat16 [1024, 5120], P('dp')
- grad_weight: bfloat16 [5120, 81920], P('dp', 'tensor')
Inputs may be any that keep to these rules, and one draw needn't show every extreme that they name: `hidden`: activations entering the head. `head_weight`: weights of the head. `prompt_ids`: ids counted in a row's prompt; an id may stand in several slots of a row, and its counts then add. `sampled_ids`: ids sampled at a row's positions.
All inputs are finite; a program needn't handle non-finite values. No bound on the sum of `token_mask` on one device may be relied on, other than what follows from the above.
Results may differ from a plain program's by a relative error of at most 0.009.
Values may be sent and summed in bfloat16 or wider, within the bound.
A program may use at most 128 MiB of HBM per device.

v0:
```python
import jax
import jax.numpy as jnp
from jax import lax
from jax.sharding import PartitionSpec as P

GROUP = 8


recurrence_deduction = 0.4
presence_deduction = 0.6
division_coolness = 0.8


def penalty_tile(prompt_ids, prompt_counts, sampled_ids, vocab_offset, vocab_width):
    columns = vocab_offset + jnp.arange(vocab_width, dtype=jnp.int32)
    prompt_hits = prompt_ids[:, :, None] == columns[None, None, :]
    prompt_tile = jnp.sum(jnp.where(prompt_hits, prompt_counts[:, :, None], 0), axis=1).astype(
        jnp.float32
    )
    chosen_indicator = (sampled_ids[:, :, None] == columns[None, None, :]).astype(jnp.float32)
    resp_len = sampled_ids.shape[1]
    positions = jnp.arange(resp_len, dtype=jnp.int32)
    earlier = (positions[None, :] < positions[:, None]).astype(jnp.float32)
    prior = jnp.einsum("kq,rqv->rkv", earlier, chosen_indicator, precision=lax.Precision.HIGHEST)
    symbol_repeat_tally = prompt_tile[:, None, :] + prior
    return (symbol_repeat_tally.reshape(-1, vocab_width), chosen_indicator.reshape(-1, vocab_width))


def reduce_hidden(partial_sums):
    return lax.psum(partial_sums, "tensor").astype(jnp.bfloat16)


def shards(hidden, head_weight, prompt_ids, prompt_counts, sampled_ids, token_mask, rewards):
    tok_count = hidden.shape[0]
    slice_width = head_weight.shape[0]
    vocab_width = head_weight.shape[1]
    vocab_offset = lax.axis_index("tensor") * vocab_width
    symbol_repeat_tally, chosen_indicator = penalty_tile(
        prompt_ids, prompt_counts, sampled_ids, vocab_offset, vocab_width
    )
    group_slices = lax.all_to_all(hidden, "dp", split_axis=1, concat_axis=0, tiled=True)
    rows_part = group_slices
    lexicon_scores = lax.psum_scatter(
        jnp.dot(rows_part, head_weight, preferred_element_type=jnp.float32),
        "dp",
        scatter_dimension=0,
        tiled=True,
    )
    symbol_present_marker = (symbol_repeat_tally > 0.0).astype(jnp.float32)
    cooled_scores = (
        lexicon_scores
        - recurrence_deduction * symbol_repeat_tally
        - presence_deduction * symbol_present_marker
    ) / division_coolness
    own_top = jnp.max(cooled_scores, axis=1)
    picked_local = jnp.sum(chosen_indicator * cooled_scores, axis=1)
    row_top = lax.pmax(own_top, "tensor")
    own_total = jnp.sum(jnp.exp(cooled_scores - row_top[:, None]), axis=1)
    row_total, picked = lax.psum((own_total, picked_local), "tensor")
    normalizer = row_top + jnp.log(row_total)
    logprobs = (picked - normalizer).reshape(sampled_ids.shape)
    normalized_chances = jnp.exp(cooled_scores - normalizer[:, None])
    reward_groups = rewards.reshape(-1, GROUP)
    advantage = (reward_groups - jnp.mean(reward_groups, axis=1, keepdims=True)).reshape(-1)
    position_multiplier = (-(advantage[:, None] * token_mask.astype(jnp.float32))).reshape(-1)
    score_derivative = (
        position_multiplier[:, None] / division_coolness * (chosen_indicator - normalized_chances)
    ).astype(jnp.bfloat16)
    portion = lax.all_gather(score_derivative, "dp", axis=0, tiled=True)
    weight_acc = jnp.zeros((slice_width, vocab_width), jnp.float32)
    for block_index in range(portion.shape[0] // tok_count):
        rows_part = lax.dynamic_slice_in_dim(group_slices, block_index * tok_count, tok_count, 0)
        grad_part = portion[block_index * tok_count : (block_index + 1) * tok_count]
        partial_term = lax.dot_general(
            rows_part, grad_part, (((0,), (0,)), ((), ())), preferred_element_type=jnp.float32
        ).astype(jnp.bfloat16)
        partial_term = lax.optimization_barrier(partial_term)
        weight_acc = weight_acc + partial_term.astype(jnp.float32)
    hidden_part = lax.dot_general(
        portion, head_weight, (((1,), (1,)), ((), ())), preferred_element_type=jnp.float32
    )
    hidden_acc = hidden_part
    weight_acc, hidden_acc = (weight_acc, hidden_acc)
    grad_weight = weight_acc.astype(jnp.bfloat16)
    hidden_cols = reduce_hidden(hidden_acc)
    grad_hidden = lax.all_to_all(hidden_cols, "dp", split_axis=0, concat_axis=1, tiled=True)
    return (logprobs, grad_hidden, grad_weight)


def solution(mesh):
    return jax.shard_map(
        shards,
        mesh=mesh,
        in_specs=(
            P("dp", None),
            P("dp", "tensor"),
            P("dp", None),
            P("dp", None),
            P("dp", None),
            P("dp", None),
            P("dp"),
        ),
        out_specs=(P("dp", None), P("dp", None), P("dp", "tensor")),
        check_vma=False,
    )
```

profile of v0, /device:TPU:32, one launch (start us, length us, event | category | flops | bytes accessed | tf_op | source)
XLA Modules:
  0.0 988.6 jit_solution(10498481613659622023)
XLA Ops:
  7.2 4.5 copy.22
  11.8 35.8 %all_to_all.38 = bf16[256,4,1280]{0,2,1:T(8,128)(2,1)} all-to-all(bf16[256,4,1280]{0,2,1:T(8,128)(2,1)} %bitcast.59), channel_id=1, replica_groups=mesh['dp'=4,'tensor'=64] {'dp'}, dimensions={1} | all-to-all | bytes 5242880 | tf_op jit(solution)/shard_map/all_to_all | solution.py:41
  47.6 4.4 copy.23
  52.0 7.6 fusion.20
  61.4 2.0 broadcast_multiply_fusion
  63.5 55.4 %reduce-scatter.2.cloned.1.call-done = f32[256,1280]{1,0:T(8,128)} async-done(((f32[1024,1280]{1,0:T(8,128)}), f32[256,1280]{1,0:T(8,128)}) %reduce-scatter.2.cloned.1.call-update) | async-done | bytes 1310736 | tf_op jit(solution)/shard_map/reduce_scatter | solution.py:43
  118.9 3.3 fusion.18
  122.2 178.1 %pmax.7 = f32[256]{0:T(256)S(1)} all-reduce(f32[256]{0:T(256)S(1)} %get-tuple-element.19), channel_id=1, replica_groups=mesh['dp'=4,'tensor'=64] {'tensor'}, use_global_device_ids=true, to_apply=%region_5.6 | all-reduce | flops 256 | bytes 2048 | tf_op jit(solution)/shard_map/pmax | solution.py:57
  300.3 1.8 exponential_reduce_fusion
  302.1 182.8 %psum.22 = f32[256]{0:T(256)S(1)} all-reduce(f32[256]{0:T(256)S(1)} %get-tuple-element.15), channel_id=1, replica_groups=mesh['dp'=4,'tensor'=64] {'tensor'}, use_global_device_ids=true, to_apply=%region_7.8 | all-reduce | flops 256 | bytes 2048 | tf_op jit(solution)/shard_map/psum | solution.py:59
  484.8 2.6 fusion.7
  487.4 28.4 %all-gather.2.cloned.1.call-done = bf16[1024,1280]{1,0:T(8,128)(2,1)} async-done(((bf16[256,1280]{1,0:T(8,128)(2,1)}), bf16[1024,1280]{1,0:T(8,128)(2,1)}) %all-gather.2.cloned.1.call-update) | async-done | bytes 2621456 | tf_op jit(solution)/shard_map/all_gather | solution.py:69
  515.8 4.2 fusion.3
  520.1 4.0 fusion.2
  524.1 2.8 fusion.1
  526.9 2.9 fusion
  529.8 5.3 fusion.21
  535.1 407.1 %all-reduce.2 = (f32[256]{0:T(256)S(1)}, bf16[1024,1280]{1,0:T(8,128)(2,1)}) all-reduce(f32[256]{0:T(256)S(1)} %get-tuple-element.16, f32[1024,1280]{1,0:T(8,128)} %fusion.21), channel_id=1, replica_groups=mesh['dp'=4,'tensor'=64] {'tensor'}, use_global_device_ids=true, to_apply=%region_3.4 | all-reduce | flops 1310976 | bytes 7866368 | tf_op jit(solution)/shard_map/psum | solution.py:59
  942.3 4.5 all-to-all-start.1
  946.8 8.1 add_convert_fusion
  954.9 5.6 copy.29
  960.6 0.7 reshape.65
  961.2 16.9 %all-to-all-done.1 = bf16[4,256,1280]{2,1,0:T(8,128)(2,1)} async-done(((bf16[4,256,1280]{2,1,0:T(8,128)(2,1)}), bf16[4,256,1280]{2,1,0:T(8,128)(2,1)}, u32[]{:S(2)}, u32[]{:S(2)}) %all-to-all-start.1) | async-done | bytes 2621472 | tf_op jit(solution)/shard_map/all_to_all | solution.py:86
  978.2 3.6 copy.30
  (34 shorter events, 1.9 us)
Async XLA Ops:
  7.2 44.8 %copy-start = (bf16[1280,1280]{1,0:T(8,128)(2,1)S(1)}, bf16[1280,1280]{1,0:T(8,128)(2,1)}, u32[]{:S(2)}) copy-start(bf16[1280,1280]{1,0:T(8,128)(2,1)} %param.8) | copy-start | bytes 9830404
  7.2 111.7 %reduce-scatter.2.cloned.1.call-start = ((), (), s32[]{:S(2)}) async-start(), calls=%async_computation.3 | async-start | bytes 6553600 | tf_op jit(solution)/shard_map/reduce_scatter | solution.py:43
  59.6 0.7 copy-start.3
  59.6 0.8 copy-start.7
  59.6 1.2 copy-start.4
  59.6 1.3 copy-start.5
  59.6 1.3 copy-start.6
  59.6 456.2 %all-gather.2.cloned.1.call-start = ((), (), s32[]{:S(2)}) async-start(), calls=%async_computation.4 | async-start | bytes 3276800 | tf_op jit(solution)/shard_map/all_gather | solution.py:69
  515.8 4.2 copy-start.1
  520.1 4.0 copy-start.2
  942.3 35.9 %all-to-all-start.1 = ((bf16[4,256,1280]{2,1,0:T(8,128)(2,1)}), bf16[4,256,1280]{2,1,0:T(8,128)(2,1)}, u32[]{:S(2)}, u32[]{:S(2)}) async-start(bf16[4,256,1280]{2,1,0:T(8,128)(2,1)} %bitcast.60), calls=%async_computation.2 | async-start | bytes 5242880 | tf_op jit(solution)/shard_map/all_to_all | solution.py:86
Sparse Core Ops, SparseCore 0:
  59.7 59.1 reduce-scatter.1
  487.6 28.2 all-gather.1
where the time goes:
time: 997 us; the launch traced here: 989 us
  blocking collectives  804 us (81%)
  waiting for transfers between devices  101 us (10%)
  matrix products  28.9 us (3%)
  local copies, waits for them, and re-layouts  19.8 us (2%)
  other arithmetic  16.5 us (2%)
  between operations  14.1 us (1%)
    psum x2, blocking collectives, shards(): row_total, picked = lax.psum((own_total, picked_local), 'tensor')  590 us
    pmax x1, blocking collectives, shards(): row_top = lax.pmax(own_top, 'tensor')  178 us
    reduce_scatter x1, waiting for transfers between devices, shards(): lax.psum_scatter(jnp.dot(rows_part, head_weight, preferred_element_type=j...  55.4 us
    all_to_all x1, blocking collectives, shards(): lax.all_to_all(hidden, 'dp', split_axis=1, concat_axis=0, tiled=True)  35.8 us
    all_gather x1, waiting for transfers between devices, shards(): portion = lax.all_gather(score_derivative, 'dp', axis=0, tiled=True)  28.4 us
  transfers between devices with their start and end apart: 3, of which 3 were waited for; matrix products, arithmetic and copies ran while one was open for 2% of the time, Pallas kernels for 0%

commit v1 on v0

v1 whole, which is shorter than its diff:
```python
import functools

import jax
import jax.numpy as jnp
from jax import lax
from jax.experimental import pallas as pl
from jax.experimental.pallas import tpu as pltpu
from jax.sharding import PartitionSpec as P

GROUP = 8
NX, NZ, NY = 4, 8, 4
MESH = pl.DeviceIdType.MESH
F32, BF16 = jnp.float32, jnp.bfloat16

recurrence_deduction = 0.4
presence_deduction = 0.6
division_coolness = 0.8


class Place:
    def __init__(self):
        dp, t = lax.axis_index("dp"), lax.axis_index("tensor")
        self.ylo, self.c = dp // 2, dp % 2
        self.yhi, self.x, self.z = t // 32, (t // 8) % 4, t % 8
        self.dp = dp

    def peer(self, x=0, y=0, z=0, c=0):
        yy = (self.yhi * 2 + self.ylo + y) % NY
        xx, zz, cc = (self.x + x) % NX, (self.z + z) % NZ, (self.c + c) % 2
        return ((yy % 2) * 2 + cc, (yy // 2) * 32 + xx * 8 + zz)


def meet(peers):
    barrier = pltpu.get_barrier_semaphore()
    for who in peers:
        pl.semaphore_signal(barrier, inc=1, device_id=who, device_id_type=MESH)
    pl.semaphore_wait(barrier, len(peers))


def send(src, dst, ssem, rsem, who):
    copy = pltpu.make_async_remote_copy(
        src_ref=src, dst_ref=dst, send_sem=ssem, recv_sem=rsem, device_id=who, device_id_type=MESH
    )
    copy.start()
    return copy


Z_PEERS = [dict(z=i) for i in range(1, NZ)]
XY_PEERS = [dict(x=i, y=j) for i in range(NX) for j in (0, 2) if (i, j) != (0, 0)]


def merge(m, l, p, others):
    top = m
    for o in others:
        top = jnp.maximum(top, o[0:2])
    l = l * jnp.exp(m - top)
    for o in others:
        l = l + o[2:4] * jnp.exp(o[0:2] - top)
        p = p + o[4:6]
    return top, l, p


def stats_kernel(s_ref, o_ref, mine, land, ssem, rsem):
    me = Place()
    meet([me.peer(**s) for s in Z_PEERS + XY_PEERS])
    m, l, p = s_ref[0:2], s_ref[2:4], s_ref[4:6]
    done = []
    for stage, peers in enumerate((Z_PEERS, XY_PEERS)):
        mine[stage] = jnp.concatenate([m, l, p, jnp.zeros_like(p)], axis=0)
        copies = []
        for i, s in enumerate(peers):
            k = stage * 7 + i
            copies.append(send(mine.at[stage], land.at[k], ssem.at[k], rsem.at[k], me.peer(**s)))
        for copy in copies:
            copy.wait_recv()
        done += copies
        m, l, p = merge(m, l, p, [land[stage * 7 + i] for i in range(7)])
    o_ref[...] = jnp.concatenate([m, l, p, jnp.zeros_like(p)], axis=0)
    for copy in done:
        copy.wait_send()


def combine_stats(stats):
    return pl.pallas_call(
        stats_kernel,
        out_shape=jax.ShapeDtypeStruct((8, 128), F32),
        in_specs=[pl.BlockSpec(memory_space=pltpu.VMEM)],
        out_specs=pl.BlockSpec(memory_space=pltpu.VMEM),
        scratch_shapes=[
            pltpu.VMEM((2, 8, 128), F32),
            pltpu.VMEM((14, 8, 128), F32),
            pltpu.SemaphoreType.DMA((14,)),
            pltpu.SemaphoreType.DMA((14,)),
        ],
        compiler_params=pltpu.CompilerParams(collective_id=0, has_side_effects=True),
        name="stats",
    )(stats)


CHAINS = [(1, 0, True), (-1, 1, True), (1, 1, False), (-1, 0, False)]


class Ring:
    def __init__(self, n, at, get, out, land, ssem, rsem, ahead, behind):
        self.n, self.at, self.get, self.out, self.land = n, at, get, out, land
        self.ssem, self.rsem, self.toward = ssem, rsem, {1: ahead, -1: behind}
        self.slots, self.copies = {}, {}
        for i, (d, half, far) in enumerate(CHAINS):
            for h in range(n // 2 - (0 if far else 1)):
                self.slots[i, h] = len(self.slots)

    def hops(self, i):
        return self.n // 2 - (0 if CHAINS[i][2] else 1)

    def step(self, h):
        for i, (d, half, far) in enumerate(CHAINS):
            if h >= self.hops(i):
                continue
            chunk = (self.at + d * (self.hops(i) - h) + self.n) % self.n
            term = self.get(half, chunk)
            if h:
                self.copies[i, h - 1].wait_recv()
                term = term + self.land[self.slots[i, h - 1]].astype(F32)
            k = self.slots[i, h]
            self.out[k] = term.astype(BF16)
            self.copies[i, h] = send(
                self.out.at[k], self.land.at[k], self.ssem.at[k], self.rsem.at[k], self.toward[d]
            )

    def total(self, half):
        term = self.get(half, self.at)
        for i, (d, hf, far) in enumerate(CHAINS):
            if hf == half:
                self.copies[i, self.hops(i) - 1].wait_recv()
                term = term + self.land[self.slots[i, self.hops(i) - 1]].astype(F32)
        return term

    def finish(self):
        for copy in self.copies.values():
            copy.wait_send()


def spread_ring(n, at, rows_of, out, ssem, rsem, ahead, behind):
    copies, k = {}, 0
    toward = {1: ahead, -1: behind}
    for h in range(n // 2):
        for i, (d, half, far) in enumerate(CHAINS):
            hops = n // 2 - (0 if far else 1)
            if h >= hops:
                continue
            if h:
                copies[i, h - 1].wait_recv()
            part = rows_of((at - d * h + n) % n, half)
            copies[i, h] = send(part(out), part(out), ssem.at[k], rsem.at[k], toward[d])
            k += 1
    for i, (d, half, far) in enumerate(CHAINS):
        copies[i, n // 2 - (0 if far else 1) - 1].wait_recv()
    for copy in copies.values():
        copy.wait_send()


X_PEERS = [dict(x=i) for i in range(1, NX)]
Y_PEERS = [dict(y=i, c=j) for i in range(NY) for j in range(2) if (i, j) != (0, 0)]


def grad_hidden_kernel(
    g_ref, w_ref, o_ref, part, zout, zland, xout, xland, z2, x2, z2land, x2land, ysum, yland,
    zs, zr, xs, xr, z2s, z2r, x2s, x2r, ys, yr, as_, ar, bs, br,
):
    me = Place()
    meet([me.peer(**s) for s in Z_PEERS + X_PEERS + Y_PEERS])

    @pl.loop(0, 4)
    def _(j):
        part[j] = lax.dot_general(
            g_ref[j], w_ref[...], (((1,), (1,)), ((), ())), preferred_element_type=F32
        )

    def z_get(half, chunk):
        return part[2 * half, pl.ds(pl.multiple_of(chunk * 32, 32), 32), :]

    def x_get(half, chunk):
        return part[2 * half + 1, pl.ds(pl.multiple_of(chunk * 64, 64), 64), :]

    zring = Ring(NZ, me.z, z_get, zout, zland, zs, zr, me.peer(z=1), me.peer(z=-1))
    xring = Ring(NX, me.x, x_get, xout, xland, xs, xr, me.peer(x=1), me.peer(x=-1))
    zring.step(0)
    xring.step(0)
    xring.step(1)
    zring.step(1)

    def cut(ref, at):
        rows = pl.ds(pl.multiple_of((at // 2) * 16, 16), 16)
        return ref.at[:, rows, pl.ds(pl.multiple_of((at % 2) * 640, 128), 640)]

    later = []
    for half in range(2):
        x2[half] = xring.total(half).astype(BF16)
    x_copies = []
    for i in range(1, NZ):
        x_copies.append(
            send(cut(x2, (me.z + i) % NZ), x2land.at[i - 1], x2s.at[i - 1], x2r.at[i - 1], me.peer(z=i))
        )
    zring.step(2)
    zring.step(3)
    for half in range(2):
        z2[half] = zring.total(half).astype(BF16)
    z_copies = []
    for i in range(1, NX):
        z_copies.append(
            send(cut(z2, (me.x + i) % NX), z2land.at[i - 1], z2s.at[i - 1], z2r.at[i - 1], me.peer(x=i))
        )
    for core, (own, land, copies) in enumerate(
        ((cut(z2, me.x), z2land, z_copies), (cut(x2, me.z), x2land, x_copies))
    ):
        for copy in copies:
            copy.wait_recv()
        term = own[...].astype(F32)
        for i in range(len(copies)):
            term = term + land[i].astype(F32)
        ysum[core] = term.astype(BF16)
        later += copies

    y_copies = {}
    for i, s in enumerate(Y_PEERS):
        piece = ysum.at[(me.c + s["c"]) % 2, (me.ylo + s["y"]) % 2]
        y_copies[s["y"], s["c"]] = send(piece, yland.at[i], ys.at[i], yr.at[i], me.peer(**s))
    row = jnp.where(me.c == 0, 32 * me.z + 16 * (me.x // 2), 64 * me.x + 16 * (me.z // 2))
    col = jnp.where(me.c == 0, me.x % 2, me.z % 2) * 640
    row, col = pl.multiple_of(row, 16), pl.multiple_of(col, 128)
    for dc in range(2):
        for dy in range(2):
            pair = []
            for y in (dy, dy + 2):
                if (y, dc) == (0, 0):
                    pair.append(ysum[me.c, me.ylo].astype(F32))
                else:
                    mirror = ((NY - y) % NY, dc)
                    y_copies[mirror].wait_recv()
                    pair.append(yland[Y_PEERS.index(dict(y=mirror[0], c=mirror[1]))].astype(F32))
            owner = ((me.ylo + dy) % 2) * 2 + (me.c + dc) % 2
            o_ref[owner, pl.ds(row, 16), pl.ds(col, 640)] = (pair[0] + pair[1]).astype(BF16)
    later += list(y_copies.values())

    def place(ref, r, n, cl, w):
        return ref.at[:, pl.ds(pl.multiple_of(r, 16), n), pl.ds(pl.multiple_of(cl, 128), w)]

    @pl.when(me.c == 0)
    def _():
        copies = []
        for i in range(1, NX):
            mine = place(o_ref, row, 16, col, 640)
            copies.append(send(mine, mine, as_.at[i - 1], ar.at[i - 1], me.peer(x=i)))
        for copy in copies:
            copy.wait_recv()
        spread_ring(
            NZ, me.z, lambda chunk, half: lambda ref: place(ref, 32 * chunk + 16 * half, 16, 0, 1280),
            o_ref, bs, br, me.peer(z=1), me.peer(z=-1),
        )
        for copy in copies:
            copy.wait_send()

    @pl.when(me.c == 1)
    def _():
        copies = []
        for i in range(1, NZ):
            mine = place(o_ref, row, 16, col, 640)
            copies.append(send(mine, mine, as_.at[i - 1], ar.at[i - 1], me.peer(z=i)))
        for copy in copies:
            copy.wait_recv()
        spread_ring(
            NX, me.x, lambda chunk, half: lambda ref: place(ref, 64 * chunk + 32 * half, 32, 0, 1280),
            o_ref, bs, br, me.peer(x=1), me.peer(x=-1),
        )
        for copy in copies:
            copy.wait_send()

    zring.finish()
    xring.finish()
    for copy in later:
        copy.wait_send()


def grad_hidden_of(grads, head_weight):
    vmem = pl.BlockSpec(memory_space=pltpu.VMEM)
    dma = lambda n: pltpu.SemaphoreType.DMA((n,))
    out = pl.pallas_call(
        grad_hidden_kernel,
        out_shape=jax.ShapeDtypeStruct((4, 256, 1280), BF16),
        in_specs=[vmem, vmem],
        out_specs=vmem,
        scratch_shapes=[
            pltpu.VMEM((4, 256, 1280), F32),
            pltpu.VMEM((14, 32, 1280), BF16),
            pltpu.VMEM((14, 32, 1280), BF16),
            pltpu.VMEM((6, 64, 1280), BF16),
            pltpu.VMEM((6, 64, 1280), BF16),
            pltpu.VMEM((2, 32, 1280), BF16),
            pltpu.VMEM((2, 64, 1280), BF16),
            pltpu.VMEM((3, 2, 16, 640), BF16),
            pltpu.VMEM((7, 2, 16, 640), BF16),
            pltpu.VMEM((2, 2, 16, 640), BF16),
            pltpu.VMEM((7, 16, 640), BF16),
            dma(14), dma(14), dma(6), dma(6), dma(3), dma(3), dma(7), dma(7), dma(7), dma(7),
            dma(7), dma(7), dma(14), dma(14),
        ],
        compiler_params=pltpu.CompilerParams(
            collective_id=1, has_side_effects=True, vmem_limit_bytes=50 << 20
        ),
        name="grad_hidden",
    )(grads.reshape(4, 256, 1280), head_weight)
    return jnp.transpose(out, (1, 0, 2)).reshape(256, 5120)


def penalty_tile(prompt_ids, prompt_counts, sampled_ids, vocab_offset, vocab_width):
    columns = vocab_offset + jnp.arange(vocab_width, dtype=jnp.int32)
    prompt_hits = prompt_ids[:, :, None] == columns[None, None, :]
    prompt_tile = jnp.sum(jnp.where(prompt_hits, prompt_counts[:, :, None], 0), axis=1).astype(F32)
    chosen_indicator = (sampled_ids[:, :, None] == columns[None, None, :]).astype(F32)
    resp_len = sampled_ids.shape[1]
    positions = jnp.arange(resp_len, dtype=jnp.int32)
    earlier = (positions[None, :] < positions[:, None]).astype(F32)
    prior = jnp.einsum("kq,rqv->rkv", earlier, chosen_indicator, precision=lax.Precision.HIGHEST)
    symbol_repeat_tally = prompt_tile[:, None, :] + prior
    return (symbol_repeat_tally.reshape(-1, vocab_width), chosen_indicator.reshape(-1, vocab_width))


def shards(hidden, head_weight, prompt_ids, prompt_counts, sampled_ids, token_mask, rewards):
    vocab_width = head_weight.shape[1]
    vocab_offset = lax.axis_index("tensor") * vocab_width
    symbol_repeat_tally, chosen_indicator = penalty_tile(
        prompt_ids, prompt_counts, sampled_ids, vocab_offset, vocab_width
    )
    group_slices = lax.all_to_all(hidden, "dp", split_axis=1, concat_axis=0, tiled=True)
    lexicon_scores = lax.psum_scatter(
        jnp.dot(group_slices, head_weight, preferred_element_type=F32),
        "dp",
        scatter_dimension=0,
        tiled=True,
    )
    symbol_present_marker = (symbol_repeat_tally > 0.0).astype(F32)
    cooled_scores = (
        lexicon_scores
        - recurrence_deduction * symbol_repeat_tally
        - presence_deduction * symbol_present_marker
    ) / division_coolness
    own_top = jnp.max(cooled_scores, axis=1)
    picked_local = jnp.sum(chosen_indicator * cooled_scores, axis=1)
    own_total = jnp.sum(jnp.exp(cooled_scores - own_top[:, None]), axis=1)
    stats = jnp.concatenate([own_top, own_total, picked_local, jnp.zeros_like(own_top)]).reshape(8, 128)
    stats = combine_stats(stats).reshape(4, 256)
    normalizer = stats[0] + jnp.log(stats[1])
    logprobs = (stats[2] - normalizer).reshape(sampled_ids.shape)
    normalized_chances = jnp.exp(cooled_scores - normalizer[:, None])
    reward_groups = rewards.reshape(-1, GROUP)
    advantage = (reward_groups - jnp.mean(reward_groups, axis=1, keepdims=True)).reshape(-1)
    position_multiplier = (-(advantage[:, None] * token_mask.astype(F32))).reshape(-1)
    score_derivative = (
        position_multiplier[:, None] / division_coolness * (chosen_indicator - normalized_chances)
    ).astype(BF16)
    portion = lax.all_gather(score_derivative, "dp", axis=0, tiled=True)
    grad_weight = lax.dot_general(
        group_slices, portion, (((0,), (0,)), ((), ())), preferred_element_type=F32
    ).astype(BF16)
    grad_hidden = grad_hidden_of(portion, head_weight)
    return (logprobs, grad_hidden, grad_weight)


def solution(mesh):
    return jax.shard_map(
        shards,
        mesh=mesh,
        in_specs=(
            P("dp", None),
            P("dp", "tensor"),
            P("dp", None),
            P("dp", None),
            P("dp", None),
            P("dp", None),
            P("dp"),
        ),
        out_specs=(P("dp", None), P("dp", None), P("dp", "tensor")),
        check_vma=False,
    )
```

time: 997 us -> 272 us (0.27)
  blocking collectives: 804 us -> 34.9 us
  Pallas kernels: 0 us -> 93.1 us
  waiting for transfers between devices: 101 us -> 87.9 us
  matrix products: 28.9 us -> 16.3 us
  other arithmetic: 16.5 us -> 5.85 us
    psum x2 -> x0, blocking collectives: 590 us -> none  [shards(): row_total, picked = lax.psum((own_total, picked_local), 'tensor')]
    pmax x1 -> x0, blocking collectives: 178 us -> none  [shards(): row_top = lax.pmax(own_top, 'tensor')]
    pallas_call x0 -> x2, Pallas kernels: none -> 93.1 us  [the longest x1 76.6 us: grad_hidden_of(): pl.pallas_call(grad_hidden_kernel, out_shape=jax.ShapeDtypeStruct((4, 256...]
    all_to_all x1 -> x0, waiting for transfers between devices: 16.9 us -> none  [shards(): lax.all_to_all(hidden_cols, 'dp', split_axis=0, concat_axis=1, tiled=True)]
    dot_general x6 -> x2, matrix products: 26.9 us -> 14.7 us  [the longest x1 8.58 us: shards(): jnp.dot(group_slices, head_weight, preferred_element_type=F32)]
  transfers between devices with their start and end apart: 3 -> 2, of which waited for: 3 -> 2; matrix products, arithmetic and copies ran while one was open for 2% -> 1% of each run, Pallas kernels for 0% -> 0%
where the time goes in v1:
time: 272 us; the launch traced here: 271 us
  Pallas kernels  93.1 us (34%)
  waiting for transfers between devices  87.9 us (32%)
  blocking collectives  34.9 us (13%)
  local copies, waits for them, and re-layouts  18.9 us (7%)
  matrix products  16.3 us (6%)
  between operations  14.1 us (5%)
  other arithmetic  5.85 us (2%)
    pallas_call x1, Pallas kernels, grad_hidden_of(): pl.pallas_call(grad_hidden_kernel, out_shape=jax.ShapeDtypeStruct((4, 256...  76.6 us
    reduce_scatter x1, waiting for transfers between devices, shards(): lax.psum_scatter(jnp.dot(group_slices, head_weight, preferred_element_typ...  55.8 us
    all_to_all x1, blocking collectives, shards(): lax.all_to_all(hidden, 'dp', split_axis=1, concat_axis=0, tiled=True)  34.9 us
    all_gather x1, waiting for transfers between devices, shards(): portion = lax.all_gather(score_derivative, 'dp', axis=0, tiled=True)  32.1 us
    pallas_call x1, Pallas kernels, combine_stats(): pl.pallas_call(stats_kernel, out_shape=jax.ShapeDtypeStruct((8, 128), F32...  16.5 us
    unnamed x13, local copies, waits for them, and re-layouts  12.6 us
    dot_general x1, matrix products, shards(): jnp.dot(group_slices, head_weight, preferred_element_type=F32)  8.58 us
    dot_general x1, matrix products, shards(): lax.dot_general(group_slices, portion, (((0,), (0,)), ((), ())), preferre...  6.14 us
  transfers between devices with their start and end apart: 2, of which 2 were waited for; matrix products, arithmetic and copies ran while one was open for 1% of the time, Pallas kernels for 0%

profile of v1, /device:TPU:32, one launch (start us, length us, event | category | flops | bytes accessed | tf_op | source)
XLA Modules:
  0.0 271.4 jit_solution(9723365296568463116)
XLA Ops:
  7.2 4.4 %copy.19 = bf16[256,5120]{0,1:T(8,128)(2,1)} copy(bf16[256,5120]{1,0:T(8,128)(2,1)} %param.7) | data formatting | bytes 5242880 | tf_op args[0]
  11.6 34.9 %all_to_all.19 = bf16[256,4,1280]{0,2,1:T(8,128)(2,1)S(1)} all-to-all(bf16[256,4,1280]{0,2,1:T(8,128)(2,1)} %bitcast.39), channel_id=1, replica_groups=mesh['dp'=4,'tensor'=64] {'dp'}, dimensions={1} | all-to-all | bytes 5242880 | tf_op jit(solution)/shard_map/all_to_all | solution.py:334
  46.5 2.6 copy.20
  49.1 8.6 %fusion.14 = f32[1024,1280]{1,0:T(8,128)} fusion(bf16[1024,1280]{1,0:T(8,128)(2,1)} %bitcast.40, bf16[1280,1280]{1,0:T(8,128)(2,1)} %w_ref.1), kind=kOutput, calls=%fused_computation.29 | convolution fusion | flops 3355443200 | bytes 11141120 | tf_op jit(solution)/shard_map/dot_general | solution.py:336
  57.7 0.2 all-gather.2.cloned.1.call-start
  58.0 0.4 copy-done.2
  58.4 0.5 select_reduce_fusion
  59.1 0.1 reduce_sum.39
  59.3 0.1 sub.51
  59.6 1.6 broadcast_multiply_fusion
  61.2 55.8 %reduce-scatter.2.cloned.1.call-done = f32[256,1280]{1,0:T(8,128)} async-done(((f32[1024,1280]{1,0:T(8,128)}), f32[256,1280]{1,0:T(8,128)}) %reduce-scatter.2.cloned.1.call-update) | async-done | bytes 1310736 | tf_op jit(solution)/shard_map/reduce_scatter | solution.py:335
  117.0 2.0 fusion.12
  118.9 0.4 exponential_reduce_fusion
  119.4 0.7 maximum_maximum_fusion.s_ref
  120.0 16.5 %stats.1 = f32[8,128]{1,0:T(8,128)} custom-call(f32[8,128]{1,0:T(8,128)} %maximum_maximum_fusion.s_ref), custom_call_target="tpu_custom_call" | custom-call | tf_op jit(solution)/shard_map/stats/pallas_call | solution.py:84
  136.6 0.8 fusion.11
  137.4 1.2 fusion.4
  138.6 0.7 sub.49
  139.3 32.1 %all-gather.2.cloned.1.call-done = bf16[1024,1280]{1,0:T(8,128)(2,1)} async-done(((bf16[256,1280]{1,0:T(8,128)(2,1)}), bf16[1024,1280]{1,0:T(8,128)(2,1)}) %all-gather.2.cloned.1.call-update) | async-done | bytes 2621456 | tf_op jit(solution)/shard_map/all_gather | solution.py:361
  171.4 6.1 %fusion = bf16[1280,1280]{0,1:T(8,128)(2,1)S(1)} fusion(bf16[1024,1280]{1,0:T(8,128)(2,1)} %all-gather.2.cloned.1.call-done, bf16[1024,1280]{1,0:T(8,128)(2,1)} %bitcast.41), kind=kOutput, calls=%fused_computation.1 | convolution fusion | flops 3357081600 | bytes 8519680 | tf_op jit(solution)/shard_map/dot_general | solution.py:362
  177.6 3.4 %copy.23 = bf16[1280,1280]{1,0:T(8,128)(2,1)} copy(bf16[1280,1280]{0,1:T(8,128)(2,1)S(1)} %fusion) | data formatting | bytes 6553600
  180.9 76.6 %grad_hidden.1 = bf16[4,256,1280]{2,1,0:T(8,128)(2,1)S(1)} custom-call(bf16[4,256,1280]{2,1,0:T(8,128)(2,1)} %bitcast.42, bf16[1280,1280]{1,0:T(8,128)(2,1)} %w_ref.1), custom_call_target="tpu_custom_call" | custom-call | tf_op jit(solution)/shard_map/grad_hidden/pallas_call | solution.py:287
  257.6 2.6 copy.21
  260.1 4.4 %copy.22 = bf16[256,5120]{1,0:T(8,128)(2,1)} copy(bf16[256,5120]{0,1:T(8,128)(2,1)} %bitcast.38) | data formatting | bytes 5242880
  (23 shorter events, 0.6 us)
Async XLA Ops:
  7.2 109.8 %reduce-scatter.2.cloned.1.call-start = ((), (), s32[]{:S(2)}) async-start(), calls=%async_computation.2 | async-start | bytes 6553600 | tf_op jit(solution)/shard_map/reduce_scatter | solution.py:335
  57.7 0.7 copy-start.2
  57.7 0.7 copy-start.3
  57.7 1.2 copy-start
  57.7 1.3 copy-start.4
  57.7 1.7 copy-start.1
  57.7 113.7 %all-gather.2.cloned.1.call-start = ((), (), s32[]{:S(2)}) async-start(), calls=%async_computation.3 | async-start | bytes 3276800 | tf_op jit(solution)/shard_map/all_gather | solution.py:361
Sparse Core Ops, SparseCore 0:
  57.8 59.0 reduce-scatter.1
  138.8 32.6 all-gather.1

commit v2 on v1

v2 whole, which is shorter than its diff:
```python
import functools

import jax
import jax.numpy as jnp
from jax import lax
from jax.experimental import pallas as pl
from jax.experimental.pallas import tpu as pltpu
from jax.sharding import PartitionSpec as P

GROUP = 8
NX, NZ, NY = 4, 8, 4
MESH = pl.DeviceIdType.MESH
F32, BF16 = jnp.float32, jnp.bfloat16

recurrence_deduction = 0.4
presence_deduction = 0.6
division_coolness = 0.8


class Place:
    def __init__(self):
        dp, t = lax.axis_index("dp"), lax.axis_index("tensor")
        self.ylo, self.c = dp // 2, dp % 2
        self.yhi, self.x, self.z = t // 32, (t // 8) % 4, t % 8
        self.dp = dp

    def peer(self, x=0, y=0, z=0, c=0):
        yy = (self.yhi * 2 + self.ylo + y + NY) % NY
        xx, zz, cc = (self.x + x + NX) % NX, (self.z + z + NZ) % NZ, (self.c + c) % 2
        return ((yy % 2) * 2 + cc, (yy // 2) * 32 + xx * 8 + zz)


def meet(peers):
    barrier = pltpu.get_barrier_semaphore()
    for who in peers:
        pl.semaphore_signal(barrier, inc=1, device_id=who, device_id_type=MESH)
    pl.semaphore_wait(barrier, len(peers))


def send(src, dst, ssem, rsem, who):
    copy = pltpu.make_async_remote_copy(
        src_ref=src, dst_ref=dst, send_sem=ssem, recv_sem=rsem, device_id=who, device_id_type=MESH
    )
    copy.start()
    return copy


Z_PEERS = [dict(z=i) for i in range(1, NZ)]
X_PEERS = [dict(x=i) for i in range(1, NX)]
Y_PEERS = [dict(y=i, c=j) for i in range(NY) for j in range(2) if (i, j) != (0, 0)]
XY_PEERS = [dict(x=i, y=j) for i in range(NX) for j in (0, 2) if (i, j) != (0, 0)]
ALL_PEERS = Z_PEERS + X_PEERS + Y_PEERS + [dict(x=i, y=2) for i in range(1, NX)]

WIDE, VOCAB, OWN, ALL = 1280, 1280, 256, 1024
STEP, STEPS = 32, 8
DIRECT = (1, 3)
EARLY, LATE = 0, 1
CHAINS = [(1, EARLY, True), (-1, LATE, True), (1, LATE, False), (-1, EARLY, False)]


def al(i, n):
    return pl.multiple_of(i, n)


class Ring:
    def __init__(self, n, at, get, out, land, ssem, rsem, ahead, behind):
        self.n, self.at, self.get, self.out, self.land = n, at, get, out, land
        self.ssem, self.rsem, self.toward = ssem, rsem, {1: ahead, -1: behind}
        self.slots, self.copies = {}, {}
        for i in range(len(CHAINS)):
            for h in range(self.hops(i)):
                self.slots[i, h] = len(self.slots)

    def hops(self, i):
        return self.n // 2 - (0 if CHAINS[i][2] else 1)

    def step(self, h, halves=(EARLY, LATE)):
        for i, (d, half, far) in enumerate(CHAINS):
            if h >= self.hops(i) or half not in halves:
                continue
            chunk = (self.at + d * (self.hops(i) - h) + self.n) % self.n
            term = self.get(half, chunk)
            if h:
                self.copies[i, h - 1].wait_recv()
                term = term + self.land[self.slots[i, h - 1]].astype(F32)
            k = self.slots[i, h]
            self.out[k] = term.astype(BF16)
            self.copies[i, h] = send(
                self.out.at[k], self.land.at[k], self.ssem.at[k], self.rsem.at[k], self.toward[d]
            )

    def total(self, half):
        term = self.get(half, self.at)
        for i, (d, hf, far) in enumerate(CHAINS):
            if hf == half:
                self.copies[i, self.hops(i) - 1].wait_recv()
                term = term + self.land[self.slots[i, self.hops(i) - 1]].astype(F32)
        return term

    def finish(self):
        for copy in self.copies.values():
            copy.wait_send()


def spread_ring(n, at, part, ssem, rsem, ahead, behind, between):
    copies, k = {}, 0
    toward = {1: ahead, -1: behind}
    for h in range(n // 2):
        for i, (d, half, far) in enumerate(CHAINS):
            hops = n // 2 - (0 if far else 1)
            if h >= hops:
                continue
            if h:
                copies[i, h - 1].wait_recv()
            piece = part((at - d * h + n) % n, half)
            copies[i, h] = send(piece, piece, ssem.at[k], rsem.at[k], toward[d])
            k += 1
        between(h)
    for i, (d, half, far) in enumerate(CHAINS):
        copies[i, n // 2 - (0 if far else 1) - 1].wait_recv()
    for copy in copies.values():
        copy.wait_send()


def merge(m, l, p, others):
    top = m
    for o in others:
        top = jnp.maximum(top, o[0:1])
    l = l * jnp.exp(m - top)
    for o in others:
        l = l + o[1:2] * jnp.exp(o[0:1] - top)
        p = p + o[2:3]
    return top, l, p


def rows_of(i, n):
    return pl.ds(al(i, n), n)


def kernel(
    hid_ref, w_hbm, pen_hbm, ids_ref, tw_ref, lp_ref, gh_ref, gw_ref,
    w_ref, pen_ref, hd, lex, pout, pland, xout, xland, lout, lland, chosen_ref, st, mine, sland,
    gr, part, zout, zland, xrout, xrland, z2, x2, z2land, x2land, ysum, yland, gather,
    loc, hs, hr, cs, cr, ps, pr, xs, xr, ls, lr, ss, sr, gs, grs,
    zs, zr, xrs, xrr, z2s, z2r, x2s, x2r, ys, yr, as_, ar, bs, br,
):
    me = Place()
    toward = 1 - 2 * me.ylo
    mate, across = me.peer(c=1), me.peer(y=toward)
    other = 2 * (1 - me.ylo)
    own, mates = me.dp, 2 * me.ylo + 1 - me.c

    copy_w = pltpu.make_async_copy(w_hbm, w_ref, loc.at[0])
    copy_h = pltpu.make_async_copy(
        hid_ref.at[:, pl.ds(al(own * WIDE, 128), WIDE)], hd.at[rows_of(own * OWN, OWN)], loc.at[1]
    )
    copy_p = pltpu.make_async_copy(pen_hbm, pen_ref, loc.at[2])
    copy_w.start()
    copy_h.start()
    copy_p.start()
    meet([me.peer(**s) for s in ALL_PEERS])

    def hidden_copy(rel, step, way):
        who = me.peer(y=way, c=rel)
        to = other + (me.c + rel) % 2
        k = rel * STEPS + step
        return pltpu.make_async_remote_copy(
            src_ref=hid_ref.at[rows_of(step * STEP, STEP), pl.ds(al(to * WIDE, 128), WIDE)],
            dst_ref=hd.at[rows_of(own * OWN + step * STEP, STEP)],
            send_sem=hs.at[k],
            recv_sem=hr.at[k],
            device_id=who,
            device_id_type=MESH,
        )

    to_mate = send(
        hid_ref.at[:, pl.ds(al(mates * WIDE, 128), WIDE)], hd.at[rows_of(own * OWN, OWN)],
        cs.at[0], cr.at[0], mate,
    )
    wrapped = [s for s in range(STEPS) if s not in DIRECT]
    hidden = {}
    for s in range(STEPS):
        for rel in range(2):
            hidden[rel, s] = hidden_copy(rel, s, toward if s in DIRECT else -toward)
    ahead = 2
    for s in DIRECT[:1] + tuple(wrapped[:ahead]) + DIRECT[1:]:
        for rel in range(2):
            hidden[rel, s].start()

    copy_w.wait()
    copy_h.wait()
    to_mate.wait_recv()

    @pl.loop(0, 4)
    def _(i):
        at = rows_of(mates * OWN + i * 64, 64)
        pout[rows_of(i * 64, 64)] = jnp.dot(hd[at, :], w_ref[...], preferred_element_type=F32)

    to_mate_part = send(pout, pland, ps.at[0], pr.at[0], mate)
    mine_of, mates_of = other + me.c, other + 1 - me.c
    exchanged, crossed = [], []
    for s in range(STEPS):
        for rel in range(2):
            hidden[rel, s].wait_recv()
        both = jnp.concatenate(
            [hd[rows_of(mates_of * OWN + s * STEP, STEP), :], hd[rows_of(mine_of * OWN + s * STEP, STEP), :]], axis=0
        )
        term = jnp.dot(both, w_ref[...], preferred_element_type=F32)
        xout[s] = term[:STEP]
        exchanged.append(send(xout.at[s], xland.at[s], xs.at[s], xr.at[s], mate))
        if s in wrapped:
            i = wrapped.index(s) + ahead
            if i < len(wrapped):
                for rel in range(2):
                    hidden[rel, wrapped[i]].start()
        exchanged[s].wait_recv()
        lout[s] = term[STEP:] + xland[s]
        crossed.append(send(lout.at[s], lland.at[s], ls.at[s], lr.at[s], across))
        if s == 1:

            @pl.loop(0, 4)
            def _(i):
                lex[rows_of(i * 64, 64)] = jnp.dot(
                    hd[rows_of(own * OWN + i * 64, 64), :], w_ref[...], preferred_element_type=F32
                )

    copy_p.wait()
    to_mate_part.wait_recv()
    lane = lax.broadcasted_iota(jnp.int32, (STEP, 128), 1)
    column = lax.broadcasted_iota(jnp.int32, (STEP, VOCAB), 1)
    for s in range(STEPS):
        crossed[s].wait_recv()
        at = pl.ds(s * STEP, STEP)
        scaled = (lex[at, :] + pland[at, :] + lland[s] - pen_ref[at, :]) * 1.25
        lex[at, :] = scaled
        chosen = column == ids_ref[at, :]
        m = jnp.max(scaled, axis=1, keepdims=True)
        l = jnp.sum(jnp.exp(scaled - m), axis=1, keepdims=True)
        p = jnp.sum(jnp.where(chosen, scaled, 0.0), axis=1, keepdims=True)
        st[at, :] = jnp.where(lane == 0, m, jnp.where(lane == 1, l, jnp.where(lane == 2, p, 0.0)))
    across_rows = st[...].T[0:8]
    m, l, p = across_rows[0:1], across_rows[1:2], across_rows[2:3]
    stats = []
    for stage, peers in enumerate((Z_PEERS, XY_PEERS)):
        mine[stage] = across_rows
        copies = []
        for i, s in enumerate(peers):
            k = stage * 7 + i
            copies.append(send(mine.at[stage], sland.at[k], ss.at[k], sr.at[k], me.peer(**s)))
        for copy in copies:
            copy.wait_recv()
        stats += copies
        m, l, p = merge(m, l, p, [sland[stage * 7 + i] for i in range(7)])
        across_rows = jnp.concatenate([m, l, p, jnp.zeros((5, OWN), F32)], axis=0)
    norm = m + jnp.log(l)
    lp_ref[...] = jnp.broadcast_to(p - norm, (8, OWN))
    st[...] = jnp.broadcast_to(norm, (128, OWN)).T

    for s in range(STEPS):
        at = pl.ds(s * STEP, STEP)
        chosen = jnp.where(column == ids_ref[at, :], 1.0, 0.0)
        g = tw_ref[at, :] * (chosen - jnp.exp(lex[at, :] - st[at, 0:1]))
        gr[rows_of(own * OWN + s * STEP, STEP)] = g.astype(BF16)
    grads = {}

    def grad_send(k, j, half, who):
        at = rows_of(j * OWN + half * 128, 128)
        grads[k] = send(gr.at[at], gr.at[at], gs.at[k], grs.at[k], who)

    for half in range(2):
        grad_send(half, own, half, across)
    for half in range(2):
        grad_send(2 + half, own, half, mate)

    def product(j):
        part[j] = lax.dot_general(
            gr[rows_of(j * OWN, OWN), :], w_ref[...], (((1,), (1,)), ((), ())), preferred_element_type=F32
        )

    def relay(half):
        grads[half].wait_recv()
        grad_send(4 + half, mine_of, half, mate)

    def z_get(half, chunk):
        ylo = me.ylo if half == EARLY else 1 - me.ylo
        return part[2 * ylo, rows_of(chunk * 32, 32), :]

    def x_get(half, chunk):
        ylo = me.ylo if half == EARLY else 1 - me.ylo
        return part[2 * ylo + 1, rows_of(chunk * 64, 64), :]

    zring = Ring(NZ, me.z, z_get, zout, zland, zs, zr, me.peer(z=1), me.peer(z=-1))
    xring = Ring(NX, me.x, x_get, xrout, xrland, xrs, xrr, me.peer(x=1), me.peer(x=-1))
    grads[2].wait_recv()
    grads[3].wait_recv()

    @pl.loop(0, 2)
    def _(i):
        product(2 * me.ylo + i)

    E, L = (EARLY,), (LATE,)
    zring.step(0, E)
    xring.step(0, E)
    zring.step(1, E)
    xring.step(1, E)
    relay(0)
    zring.step(2, E)
    relay(1)
    zring.step(3, E)
    grads[4].wait_recv()
    grads[5].wait_recv()

    @pl.loop(0, 2)
    def _(i):
        product(other + i)

    zring.step(0, L)
    xring.step(0, L)
    zring.step(1, L)
    xring.step(1, L)
    zring.step(2, L)

    def weight_tiles(lo, hi):
        @pl.loop(lo, hi)
        def _(i):
            cols = pl.ds(al(i * 128, 128), 128)
            gw_ref[cols, :] = lax.dot_general(
                hd[:, cols], gr[...], (((0,), (0,)), ((), ())), preferred_element_type=F32
            ).astype(BF16)

    def cut(ref, at):
        rows = rows_of((at // 2) * 16, 16)
        return ref.at[:, rows, pl.ds(al((at % 2) * 640, 128), 640)]

    later = []
    x2[me.ylo] = xring.total(EARLY).astype(BF16)
    x2[1 - me.ylo] = xring.total(LATE).astype(BF16)
    x_copies = []
    for i in range(1, NZ):
        x_copies.append(
            send(cut(x2, (me.z + i) % NZ), x2land.at[i - 1], x2s.at[i - 1], x2r.at[i - 1], me.peer(z=i))
        )
    zring.step(3, L)
    z2[me.ylo] = zring.total(EARLY).astype(BF16)
    z2[1 - me.ylo] = zring.total(LATE).astype(BF16)
    z_copies = []
    for i in range(1, NX):
        z_copies.append(
            send(cut(z2, (me.x + i) % NX), z2land.at[i - 1], z2s.at[i - 1], z2r.at[i - 1], me.peer(x=i))
        )
    weight_tiles(0, 2)
    for core, (ours, land, copies) in enumerate(
        ((cut(z2, me.x), z2land, z_copies), (cut(x2, me.z), x2land, x_copies))
    ):
        for copy in copies:
            copy.wait_recv()
        term = ours[...].astype(F32)
        for i in range(len(copies)):
            term = term + land[i].astype(F32)
        ysum[core] = term.astype(BF16)
        later += copies

    y_copies = {}
    for i, s in enumerate(Y_PEERS):
        piece = ysum.at[(me.c + s["c"]) % 2, (me.ylo + s["y"]) % 2]
        y_copies[s["y"], s["c"]] = send(piece, yland.at[i], ys.at[i], yr.at[i], me.peer(**s))
    weight_tiles(2, 4)
    row = jnp.where(me.c == 0, 32 * me.z + 16 * (me.x // 2), 64 * me.x + 16 * (me.z // 2))
    col = jnp.where(me.c == 0, me.x % 2, me.z % 2) * 640
    kept = lambda: (slice(None), rows_of(row, 16), pl.ds(al(col, 128), 640))
    for dc in range(2):
        for dy in range(2):
            pair = []
            for y in (dy, dy + 2):
                if (y, dc) == (0, 0):
                    pair.append(ysum[me.c, me.ylo].astype(F32))
                else:
                    mirror = ((NY - y) % NY, dc)
                    y_copies[mirror].wait_recv()
                    pair.append(yland[Y_PEERS.index(dict(y=mirror[0], c=mirror[1]))].astype(F32))
            owner = ((me.ylo + dy) % 2) * 2 + (me.c + dc) % 2
            gather[owner, rows_of(row, 16), pl.ds(al(col, 128), 640)] = (pair[0] + pair[1]).astype(BF16)
    later += list(y_copies.values())

    def gather_all(first, first_sems, ring, n, at, part_of, ahead, behind):
        copies = []
        for i, s in enumerate(first):
            piece = gather.at[kept()]
            copies.append(send(piece, piece, as_.at[i], ar.at[i], me.peer(**s)))
        weight_tiles(4, 6)
        for copy in copies:
            copy.wait_recv()
        spread_ring(n, at, part_of, bs, br, ahead, behind, lambda h: weight_tiles(6 + 2 * h, 8 + 2 * h) if h < 2 else None)
        for copy in copies:
            copy.wait_send()

    @pl.when(me.c == 0)
    def _():
        gather_all(
            X_PEERS, None, None, NZ, me.z,
            lambda chunk, half: gather.at[:, rows_of(32 * chunk + 16 * half, 16), :],
            me.peer(z=1), me.peer(z=-1),
        )

    @pl.when(me.c == 1)
    def _():
        gather_all(
            Z_PEERS, None, None, NX, me.x,
            lambda chunk, half: gather.at[:, rows_of(64 * chunk + 32 * half, 32), :],
            me.peer(x=1), me.peer(x=-1),
        )

    outs = []
    for s in range(4):
        copy = pltpu.make_async_copy(gather.at[s], gh_ref.at[:, pl.ds(s * WIDE, WIDE)], loc.at[3 + s])
        copy.start()
        outs.append(copy)
    zring.finish()
    xring.finish()
    to_mate.wait_send()
    to_mate_part.wait_send()
    for copy in later + exchanged + crossed + stats + list(hidden.values()) + list(grads.values()):
        copy.wait_send()
    for copy in outs:
        copy.wait()


def fused(hidden, head_weight, penalty, ids, weight):
    vmem = pl.BlockSpec(memory_space=pltpu.VMEM)
    hbm = pl.BlockSpec(memory_space=pl.ANY)
    dma = lambda n: pltpu.SemaphoreType.DMA((n,))
    buf = lambda *shape: pltpu.VMEM(shape, BF16)
    wide = lambda *shape: pltpu.VMEM(shape, F32)
    return pl.pallas_call(
        kernel,
        out_shape=(
            jax.ShapeDtypeStruct((8, OWN), F32),
            jax.ShapeDtypeStruct((OWN, 4 * WIDE), BF16),
            jax.ShapeDtypeStruct((WIDE, VOCAB), BF16),
        ),
        in_specs=[hbm, hbm, hbm, vmem, vmem],
        out_specs=(vmem, hbm, vmem),
        scratch_shapes=[
            buf(WIDE, VOCAB), wide(OWN, VOCAB), buf(ALL, WIDE), wide(OWN, VOCAB), wide(OWN, VOCAB), wide(OWN, VOCAB),
            wide(STEPS, STEP, VOCAB), wide(STEPS, STEP, VOCAB), wide(STEPS, STEP, VOCAB), wide(STEPS, STEP, VOCAB),
            wide(8, 128), wide(OWN, 128), wide(2, 8, OWN), wide(14, 8, OWN),
            buf(ALL, VOCAB), wide(4, OWN, WIDE),
            buf(14, 32, 1280), buf(14, 32, 1280), buf(6, 64, 1280), buf(6, 64, 1280),
            buf(2, 32, 1280), buf(2, 64, 1280), buf(3, 2, 16, 640), buf(7, 2, 16, 640), buf(2, 2, 16, 640),
            buf(7, 16, 640), buf(4, OWN, WIDE),
            dma(7), dma(16), dma(16), dma(1), dma(1), dma(1), dma(1), dma(8), dma(8), dma(8), dma(8),
            dma(14), dma(14), dma(6), dma(6),
            dma(14), dma(14), dma(6), dma(6), dma(3), dma(3), dma(7), dma(7), dma(7), dma(7),
            dma(7), dma(7), dma(14), dma(14),
        ],
        compiler_params=pltpu.CompilerParams(
            collective_id=0, has_side_effects=True, vmem_limit_bytes=56 << 20
        ),
        name="fused",
    )(hidden, head_weight, penalty, ids, weight)


def penalties(prompt_ids, prompt_counts, sampled_ids, vocab_offset, vocab_width):
    columns = vocab_offset + jnp.arange(vocab_width, dtype=jnp.int32)
    prompt_hits = prompt_ids[:, :, None] == columns[None, None, :]
    prompt_tile = jnp.sum(jnp.where(prompt_hits, prompt_counts[:, :, None], 0), axis=1).astype(F32)
    chosen = (sampled_ids[:, :, None] == columns[None, None, :]).astype(F32)
    positions = jnp.arange(sampled_ids.shape[1], dtype=jnp.int32)
    earlier = (positions[None, :] < positions[:, None]).astype(F32)
    prior = jnp.einsum("kq,rqv->rkv", earlier, chosen, precision=lax.Precision.HIGHEST)
    tally = (prompt_tile[:, None, :] + prior).reshape(-1, vocab_width)
    return recurrence_deduction * tally + presence_deduction * (tally > 0.0).astype(F32)


def shards(hidden, head_weight, prompt_ids, prompt_counts, sampled_ids, token_mask, rewards):
    vocab_width = head_weight.shape[1]
    vocab_offset = lax.axis_index("tensor") * vocab_width
    penalty = penalties(prompt_ids, prompt_counts, sampled_ids, vocab_offset, vocab_width)
    reward_groups = rewards.reshape(-1, GROUP)
    advantage = (reward_groups - jnp.mean(reward_groups, axis=1, keepdims=True)).reshape(-1)
    weight = (-(advantage[:, None] * token_mask.astype(F32))).reshape(-1, 1) / division_coolness
    ids = (sampled_ids - vocab_offset).reshape(-1, 1)
    logprobs, grad_hidden, grad_weight = fused(hidden, head_weight, penalty, ids, weight)
    return (logprobs[0].reshape(sampled_ids.shape), grad_hidden, grad_weight)


def solution(mesh):
    return jax.shard_map(
        shards,
        mesh=mesh,
        in_specs=(
            P("dp", None),
            P("dp", "tensor"),
            P("dp", None),
            P("dp", None),
            P("dp", None),
            P("dp", None),
            P("dp"),
        ),
        out_specs=(P("dp", None), P("dp", None), P("dp", "tensor")),
        check_vma=False,
    )
```

time: 272 us -> 152 us (0.56)
  waiting for transfers between devices: 87.9 us -> 0 us
  Pallas kernels: 93.1 us -> 136 us
  blocking collectives: 34.9 us -> 0 us
  matrix products: 16.3 us -> 2.25 us
  between operations: 14.1 us -> 0.66 us
  local copies, waits for them, and re-layouts: 18.9 us -> 9.06 us
    reduce_scatter x1 -> x0, waiting for transfers between devices: 55.8 us -> none  [shards(): lax.psum_scatter(jnp.dot(group_slices, head_weight, preferred_element_typ...]
    pallas_call x2 -> x1, Pallas kernels: 93.1 us -> 136 us  [fused(): pl.pallas_call(kernel, out_shape=(jax.ShapeDtypeStruct((8, OWN), F32), ja...]
    all_to_all x1 -> x0, blocking collectives: 34.9 us -> none  [shards(): lax.all_to_all(hidden, 'dp', split_axis=1, concat_axis=0, tiled=True)]
    all_gather x1 -> x0, waiting for transfers between devices: 32.1 us -> none  [shards(): portion = lax.all_gather(score_derivative, 'dp', axis=0, tiled=True)]
    dot_general x3 -> x1, matrix products: 16.3 us -> 2.25 us  [penalties(): jnp.einsum('kq,rqv->rkv', earlier, chosen, precision=lax.Precision.HIGHEST)]
    unnamed x13 -> x4, local copies, waits for them, and re-layouts: 12.6 us -> 5.26 us
  transfers between devices with their start and end apart: 2 -> 0, of which waited for: 2 -> 0; matrix products, arithmetic and copies ran while one was open for 1% -> 0% of each run, Pallas kernels for 0% -> 0%
where the time goes in v2:
time: 152 us
  Pallas kernels  136 us (89%)
  local copies, waits for them, and re-layouts  9.06 us (6%)
  other arithmetic  3.48 us (2%)
  matrix products  2.25 us (1%)
    pallas_call x1, Pallas kernels, fused(): pl.pallas_call(kernel, out_shape=(jax.ShapeDtypeStruct((8, OWN), F32), ja...  136 us
    unnamed x4, local copies, waits for them, and re-layouts  5.26 us

profile of v2, /device:TPU:32, one launch (start us, length us, event | category | flops | bytes accessed | tf_op | source)
XLA Modules:
  0.0 151.8 jit_solution(18113065507759810575)
XLA Ops:
  0.6 0.7 reshape.58
  1.4 0.1 reduce_sum.19
  1.5 0.1 sub.20
  1.6 0.1 sub.21
  1.7 0.7 sub.22
  2.3 0.8 negate_multiply_fusion
  3.1 0.7 broadcast_subtract_fusion
  3.8 1.2 select_reduce_fusion
  5.0 0.8 reshape.60.ids_ref
  5.8 0.8 div.15.tw_ref
  6.5 2.2 %select_add_fusion = f32[16,1280,16]{1,2,0:T(8,128)} fusion(s32[1280]{0:T(1024)S(1)} %iota_add_fusion, s32[16,16]{1,0:T(8,128)} %param.11, f32[16,1280]{1,0:T(8,128)S(1)} %convert_element_type.13), kind=kOutput, calls=%fused_computation.2 | convolution fusion | flops 12452096 | bytes 1398784 | tf_op jit(solution)/shard_map/kq,rqv->rkv/dot_general | solution.py:470
  8.8 136.3 %fused.1 = (f32[8,256]{1,0:T(8,128)}, bf16[256,5120]{1,0:T(8,128)(2,1)}, bf16[1280,1280]{1,0:T(8,128)(2,1)}) custom-call(bf16[256,5120]{1,0:T(8,128)(2,1)} %hid_ref.1, bf16[1280,1280]{1,0:T(8,128)(2,1)} %w_hbm.1, f32[256,1280]{1,0:T(8,128)} %bitcast.6, s32[256,1]{1,0:T(8,128)} %reshape.60.ids_ref, f32[256,1]{1,0:T(8,128)} %div.15.tw_ref), custom_call_target="tpu_custom_call" | custom-call | tf_op jit(solution)/shard_map/fused/pallas_call | solution.py:434
  145.1 0.7 slice_reduce_fusion
  145.8 0.7 reshape_squeeze.3
  146.5 0.0 copy-start
  146.5 3.6 %copy.16 = bf16[256,5120]{1,0:T(8,128)(2,1)} copy(bf16[256,5120]{1,0:T(8,128)(2,1)} %get-tuple-element.13) | data formatting | bytes 5242880
  150.0 0.0 copy-done
  150.1 1.7 %copy.17 = bf16[1280,1280]{1,0:T(8,128)(2,1)} copy(bf16[1280,1280]{1,0:T(8,128)(2,1)S(1)} %copy-done) | data formatting | bytes 6553600
  (3 shorter events, 0.0 us)
Async XLA Ops:
  146.5 3.6 %copy-start = (bf16[1280,1280]{1,0:T(8,128)(2,1)S(1)}, bf16[1280,1280]{1,0:T(8,128)(2,1)}, u32[]{:S(2)}) copy-start(bf16[1280,1280]{1,0:T(8,128)(2,1)} %get-tuple-element.14) | copy-start | bytes 9830404

commit v3 on v2

v3 whole, which is shorter than its diff:
```python
import functools

import jax
import jax.numpy as jnp
from jax import lax
from jax.experimental import pallas as pl
from jax.experimental.pallas import tpu as pltpu
from jax.sharding import PartitionSpec as P

GROUP = 8
NX, NZ, NY = 4, 8, 4
MESH = pl.DeviceIdType.MESH
F32, BF16 = jnp.float32, jnp.bfloat16

recurrence_deduction = 0.4
presence_deduction = 0.6

class Place:
    def __init__(self):
        dp, t = lax.axis_index("dp"), lax.axis_index("tensor")
        self.ylo, self.c = dp // 2, dp % 2
        self.yhi, self.x, self.z = t // 32, (t // 8) % 4, t % 8
        self.dp = dp

    def peer(self, x=0, y=0, z=0, c=0):
        yy = (self.yhi * 2 + self.ylo + y + NY) % NY
        xx, zz, cc = (self.x + x + NX) % NX, (self.z + z + NZ) % NZ, (self.c + c) % 2
        return ((yy % 2) * 2 + cc, (yy // 2) * 32 + xx * 8 + zz)


def arrive(barrier, peers):
    for who in peers:
        pl.semaphore_signal(barrier, inc=1, device_id=who, device_id_type=MESH)


def send(src, dst, ssem, rsem, who):
    copy = pltpu.make_async_remote_copy(
        src_ref=src, dst_ref=dst, send_sem=ssem, recv_sem=rsem, device_id=who, device_id_type=MESH
    )
    copy.start()
    return copy


Z_PEERS = [dict(z=i) for i in range(1, NZ)]
X_PEERS = [dict(x=i) for i in range(1, NX)]
Y_PEERS = [dict(y=i, c=j) for i in range(NY) for j in range(2) if (i, j) != (0, 0)]
XY_PEERS = [dict(x=i, y=j) for i in range(NX) for j in (0, 2) if (i, j) != (0, 0)]
ALL_PEERS = Z_PEERS + X_PEERS + Y_PEERS + [dict(x=i, y=2) for i in range(1, NX)]

WIDE, VOCAB, OWN, ALL = 1280, 1280, 256, 1024
STEP, STEPS = 32, 8
DIRECT = (1, 3)
EARLY, LATE = 0, 1
CHAINS = [(d, half, sub, (d == 1) == (sub == 0)) for half in (EARLY, LATE) for sub in range(2) for d in (1, -1)]


def al(i, n):
    return pl.multiple_of(i, n)


class Ring:
    def __init__(self, n, at, get, out, land, ssem, rsem, ahead, behind):
        self.n, self.at, self.get, self.out, self.land = n, at, get, out, land
        self.ssem, self.rsem, self.toward = ssem, rsem, {1: ahead, -1: behind}
        self.slots, self.copies = {}, {}
        for i in range(len(CHAINS)):
            for h in range(self.hops(i)):
                self.slots[i, h] = len(self.slots)

    def hops(self, i):
        return self.n // 2 - (0 if CHAINS[i][3] else 1)

    def step(self, half, h):
        for i, (d, hf, sub, far) in enumerate(CHAINS):
            if h >= self.hops(i) or hf != half:
                continue
            chunk = (self.at + d * (self.hops(i) - h) + self.n) % self.n
            term = self.get(half, sub, chunk)
            if h:
                self.copies[i, h - 1].wait_recv()
                term = term + self.land[self.slots[i, h - 1]].astype(F32)
            k = self.slots[i, h]
            self.out[k] = term.astype(BF16)
            self.copies[i, h] = send(
                self.out.at[k], self.land.at[k], self.ssem.at[k], self.rsem.at[k], self.toward[d]
            )

    def total(self, half, sub):
        term = self.get(half, sub, self.at)
        for i, (d, hf, sb, far) in enumerate(CHAINS):
            if (hf, sb) == (half, sub):
                self.copies[i, self.hops(i) - 1].wait_recv()
                term = term + self.land[self.slots[i, self.hops(i) - 1]].astype(F32)
        return term

    def finish(self):
        for copy in self.copies.values():
            copy.wait_send()


def merge(m, l, p, others):
    top = m
    for o in others:
        top = jnp.maximum(top, o[0:1])
    l = l * jnp.exp(m - top)
    for o in others:
        l = l + o[1:2] * jnp.exp(o[0:1] - top)
        p = p + o[2:3]
    return top, l, p


def rows_of(i, n):
    return pl.ds(al(i, n), n)


def kernel(
    hid_ref, w_hbm, pid_ref, pc_ref, sid_ref, mask_ref, rew_ref, lp_ref, gh_ref, gw_ref,
    w_ref, hd, lex, pout, pland, xout, xland, lout, lland, prompt, id_ref, tw_ref, st, mine, sland, tab, cols,
    raw, gr, part, zout, zland, xrout, xrland, z2, x2, z2land, x2land, ysum, yland, gather,
    loc, hs, hr, cs, cr, ps, pr, xs, xr, ls, lr, ss, sr, gs, grs, ts, tr,
    zs, zr, xrs, xrr, z2s, z2r, x2s, x2r, ys, yr, as_, ar, bs, br,
):
    me = Place()
    toward = 1 - 2 * me.ylo
    mate, across, across_mate = me.peer(c=1), me.peer(y=toward), me.peer(y=toward, c=1)
    other = 2 * (1 - me.ylo)
    own, mates = me.dp, 2 * me.ylo + 1 - me.c
    mine_of, mates_of = other + me.c, other + 1 - me.c

    copy_w = pltpu.make_async_copy(w_hbm, w_ref, loc.at[0])
    copy_h = pltpu.make_async_copy(
        hid_ref.at[:, pl.ds(al(own * WIDE, 128), WIDE)], hd.at[rows_of(own * OWN, OWN)], loc.at[1]
    )
    copy_w.start()
    copy_h.start()
    peers = [me.peer(**s) for s in ALL_PEERS]
    barrier = pltpu.get_barrier_semaphore()
    arrive(barrier, peers)

    offset = (me.yhi * 32 + me.x * 8 + me.z) * VOCAB
    column = lax.broadcasted_iota(jnp.int32, (16, VOCAB), 1) + offset
    tile = jnp.zeros((16, VOCAB), F32)
    pid, pc = pid_ref[...], pc_ref[...].astype(F32)
    for j in range(pid.shape[1]):
        tile = tile + jnp.where(pid[:, j : j + 1] == column, pc[:, j : j + 1], 0.0)
    prompt[...] = tile
    diagonal = lax.broadcasted_iota(jnp.int32, (16, 16), 0) == lax.broadcasted_iota(jnp.int32, (16, 16), 1)
    which = lax.broadcasted_iota(jnp.int32, (16, 16), 0)
    advantage = jnp.zeros((16, 16), F32)
    for g in range(16 // GROUP):
        rewards = [rew_ref[g * GROUP + r] for r in range(GROUP)]
        mean = sum(rewards[1:], rewards[0]) * (1.0 / GROUP)
        for r in range(GROUP):
            advantage = jnp.where(which == g * GROUP + r, rewards[r] - mean, advantage)
    weight = -(advantage * mask_ref[...].astype(F32)) * 1.25
    sampled = sid_ref[...].astype(F32)
    for r in range(16):
        at = pl.ds(r * 16, 16)
        for ref, rows in ((id_ref, sampled), (tw_ref, weight)):
            turned = jnp.sum(jnp.where(diagonal, rows[r : r + 1, :], 0.0), axis=1, keepdims=True)
            ref[at, :] = jnp.broadcast_to(turned, (16, 128))
    pl.semaphore_wait(barrier, len(peers))

    def hidden_copy(rel, step, way):
        who = me.peer(y=way, c=rel)
        to = other + (me.c + rel) % 2
        k = rel * STEPS + step
        return pltpu.make_async_remote_copy(
            src_ref=hid_ref.at[rows_of(step * STEP, STEP), pl.ds(al(to * WIDE, 128), WIDE)],
            dst_ref=hd.at[rows_of(own * OWN + step * STEP, STEP)],
            send_sem=hs.at[k],
            recv_sem=hr.at[k],
            device_id=who,
            device_id_type=MESH,
        )

    wrapped = [s for s in range(STEPS) if s not in DIRECT]
    hidden = {}
    for s in range(STEPS):
        for rel in range(2):
            hidden[rel, s] = hidden_copy(rel, s, toward if s in DIRECT else -toward)
    ahead = 2
    for s in (wrapped[0],) + DIRECT[:1]:
        for rel in range(2):
            hidden[rel, s].start()
    to_mate = send(
        hid_ref.at[:, pl.ds(al(mates * WIDE, 128), WIDE)], hd.at[rows_of(own * OWN, OWN)],
        cs.at[0], cr.at[0], mate,
    )
    for s in tuple(wrapped[1:ahead]) + DIRECT[1:]:
        for rel in range(2):
            hidden[rel, s].start()

    copy_w.wait()
    copy_h.wait()
    to_mate.wait_recv()

    @pl.loop(0, 4)
    def _(i):
        at = rows_of(mates * OWN + i * 64, 64)
        pout[rows_of(i * 64, 64)] = jnp.dot(hd[at, :], w_ref[...], preferred_element_type=F32)

    to_mate_part = send(pout, pland, ps.at[0], pr.at[0], mate)
    exchanged, crossed = [], []
    for s in range(STEPS):
        for rel in range(2):
            hidden[rel, s].wait_recv()
        both = jnp.concatenate(
            [hd[rows_of(mates_of * OWN + s * STEP, STEP), :], hd[rows_of(mine_of * OWN + s * STEP, STEP), :]], axis=0
        )
        term = jnp.dot(both, w_ref[...], preferred_element_type=F32)
        xout[s] = term[:STEP]
        exchanged.append(send(xout.at[s], xland.at[s], xs.at[s], xr.at[s], mate))
        if s in wrapped:
            i = wrapped.index(s) + ahead
            if i < len(wrapped):
                for rel in range(2):
                    hidden[rel, wrapped[i]].start()
        exchanged[s].wait_recv()
        lout[s] = term[STEP:] + xland[s]
        crossed.append(send(lout.at[s], lland.at[s], ls.at[s], lr.at[s], across))
        if s == 1:

            @pl.loop(0, 4)
            def _(i):
                lex[rows_of(i * 64, 64)] = jnp.dot(
                    hd[rows_of(own * OWN + i * 64, 64), :], w_ref[...], preferred_element_type=F32
                )

    grads = {}

    def grad_send(k, src, j, lo, n, who):
        grads[k] = send(src, gr.at[rows_of(j * OWN + lo, n)], gs.at[k], grs.at[k], who)

    to_mate_part.wait_recv()
    lane = lax.broadcasted_iota(jnp.int32, (STEP, 128), 1)
    vocab = (lax.broadcasted_iota(jnp.int32, (STEP, VOCAB), 1) + offset).astype(F32)
    k_of = lax.broadcasted_iota(jnp.int32, (STEP, STEP), 0)
    q_of = lax.broadcasted_iota(jnp.int32, (STEP, STEP), 1)
    earlier = jnp.where((q_of < k_of) & (q_of // 16 == k_of // 16), 1.0, 0.0).astype(BF16)
    for s in range(STEPS):
        crossed[s].wait_recv()
        at = pl.ds(s * STEP, STEP)
        chosen = vocab == id_ref[at, 0:1]
        tally = jnp.dot(earlier, jnp.where(chosen, 1.0, 0.0).astype(BF16), preferred_element_type=F32)
        tally = tally + jnp.concatenate(
            [jnp.broadcast_to(prompt[2 * s + i : 2 * s + i + 1, :], (16, VOCAB)) for i in range(2)], axis=0
        )
        penalty = recurrence_deduction * tally + jnp.where(tally > 0.0, presence_deduction, 0.0)
        scaled = (lex[at, :] + pland[at, :] + lland[s] - penalty) * 1.25
        m = jnp.max(scaled, axis=1, keepdims=True)
        raised = jnp.exp(scaled - m)
        l = jnp.sum(raised, axis=1, keepdims=True)
        p = jnp.sum(jnp.where(chosen, scaled, 0.0), axis=1, keepdims=True)
        raw[at, :] = raised.astype(BF16)
        table = jnp.zeros((STEP, 128), F32)
        for i, v in enumerate((m, l, p, id_ref[at, 0:1], tw_ref[at, 0:1])):
            table = jnp.where(lane == i, v, table)
        st[at, :] = table
        if s % 2:
            lo, n = (s - 1) * STEP, 2 * STEP
            grad_send(s // 2, raw.at[pl.ds(lo, n)], own, lo, n, across)
        if s % 4 == 3:
            lo, n = (s - 3) * STEP, 4 * STEP
            grad_send(4 + s // 4, raw.at[pl.ds(lo, n)], own, lo, n, mate)
    first = st[...].T[0:8]
    m, l, p, chosen_id, weight = [first[i : i + 1] for i in range(5)]
    own_m, across_rows = m, first
    stats = []
    for stage, where in enumerate((Z_PEERS, XY_PEERS)):
        mine[stage] = across_rows
        copies = []
        for i, s in enumerate(where):
            k = stage * 7 + i
            copies.append(send(mine.at[stage], sland.at[k], ss.at[k], sr.at[k], me.peer(**s)))
        for copy in copies:
            copy.wait_recv()
        stats += copies
        m, l, p = merge(m, l, p, [sland[stage * 7 + i] for i in range(7)])
        across_rows = jnp.concatenate([m, l, p, jnp.zeros((5, OWN), F32)], axis=0)
    norm = m + jnp.log(l)
    logp = p - norm
    lp_ref[...] = jnp.concatenate([logp[:, 16 * r : 16 * r + 16] for r in range(16)], axis=0)

    tab[own] = jnp.concatenate(
        [weight * jnp.exp(own_m - norm), weight * (1.0 - jnp.exp(logp)), chosen_id, jnp.zeros((5, OWN), F32)], axis=0
    )
    tables = [send(tab.at[own], tab.at[own], ts.at[i], tr.at[i], who) for i, who in enumerate((mate, across, across_mate))]

    def turn(j, src, base):
        wide_rows = jnp.concatenate([tab[j], jnp.zeros((120, OWN), F32)], axis=0)
        cols[...] = wide_rows.T

        @pl.loop(0, OWN // STEP)
        def _(i):
            at, to = rows_of(i * STEP, STEP), rows_of(j * OWN + i * STEP, STEP)
            g = jnp.where(
                vocab == cols[at, 2:3], cols[at, 1:2], -cols[at, 0:1] * src[rows_of(base + i * STEP, STEP), :].astype(F32)
            )
            gr[to, :] = g.astype(BF16)

        part[j] = lax.dot_general(
            gr[rows_of(j * OWN, OWN), :], w_ref[...], (((1,), (1,)), ((), ())), preferred_element_type=F32
        )

    def relay(i):
        grads[i].wait_recv()
        grad_send(6 + i, gr.at[rows_of(mine_of * OWN + i * 64, 64)], mine_of, i * 64, 64, mate)

    def z_get(half, sub, chunk):
        ylo = me.ylo if half == EARLY else 1 - me.ylo
        return part[2 * ylo, rows_of(chunk * 32 + sub * 16, 16), :]

    def x_get(half, sub, chunk):
        ylo = me.ylo if half == EARLY else 1 - me.ylo
        return part[2 * ylo + 1, rows_of(chunk * 64 + sub * 32, 32), :]

    zring = Ring(NZ, me.z, z_get, zout, zland, zs, zr, me.peer(z=1), me.peer(z=-1))
    xring = Ring(NX, me.x, x_get, xrout, xrland, xrs, xrr, me.peer(x=1), me.peer(x=-1))
    relay(0)
    relay(1)
    turn(own, raw, 0)
    grads[4].wait_recv()
    grads[5].wait_recv()
    tables[0].wait_recv()
    turn(mates, gr, mates * OWN)
    zring.step(EARLY, 0)
    xring.step(EARLY, 0)
    relay(2)
    zring.step(EARLY, 1)
    relay(3)
    xring.step(EARLY, 1)
    for copy in tables[1:]:
        copy.wait_recv()
    for i in range(4):
        grads[6 + i].wait_recv()
        grads[6 + i].wait_send()

    @pl.loop(0, 2)
    def _(i):
        turn(other + i, gr, (other + i) * OWN)

    def weight_tiles(lo, hi):
        @pl.loop(lo, hi)
        def _(i):
            at = pl.ds(al(i * 128, 128), 128)
            gw_ref[at, :] = lax.dot_general(
                hd[:, at], gr[...], (((0,), (0,)), ((), ())), preferred_element_type=F32
            ).astype(BF16)

    zring.step(LATE, 0)
    xring.step(LATE, 0)
    zring.step(EARLY, 2)
    weight_tiles(0, 1)
    zring.step(LATE, 1)
    xring.step(LATE, 1)
    zring.step(EARLY, 3)
    weight_tiles(1, 2)

    def cut(ref, at):
        rows = rows_of((at // 2) * 16, 16)
        return ref.at[:, rows, pl.ds(al((at % 2) * 640, 128), 640)]

    later = []
    zring.step(LATE, 2)
    for half, ylo in ((EARLY, me.ylo), (LATE, 1 - me.ylo)):
        for sub in range(2):
            x2[ylo, pl.ds(sub * 32, 32)] = xring.total(half, sub).astype(BF16)
    x_copies = []
    for i in range(1, NZ):
        x_copies.append(
            send(cut(x2, (me.z + i) % NZ), x2land.at[i - 1], x2s.at[i - 1], x2r.at[i - 1], me.peer(z=i))
        )
    weight_tiles(2, 3)
    zring.step(LATE, 3)
    weight_tiles(3, 5)
    for half, ylo in ((EARLY, me.ylo), (LATE, 1 - me.ylo)):
        for sub in range(2):
            z2[ylo, pl.ds(sub * 16, 16)] = zring.total(half, sub).astype(BF16)
    z_copies = []
    for i in range(1, NX):
        z_copies.append(
            send(cut(z2, (me.x + i) % NX), z2land.at[i - 1], z2s.at[i - 1], z2r.at[i - 1], me.peer(x=i))
        )
    weight_tiles(5, 7)
    for core, (ours, land, copies) in enumerate(
        ((cut(z2, me.x), z2land, z_copies), (cut(x2, me.z), x2land, x_copies))
    ):
        for copy in copies:
            copy.wait_recv()
        term = ours[...].astype(F32)
        for i in range(len(copies)):
            term = term + land[i].astype(F32)
        ysum[core] = term.astype(BF16)
        later += copies

    y_copies = {}
    for i, s in enumerate(Y_PEERS):
        piece = ysum.at[(me.c + s["c"]) % 2, (me.ylo + s["y"]) % 2]
        y_copies[s["y"], s["c"]] = send(piece, yland.at[i], ys.at[i], yr.at[i], me.peer(**s))
    weight_tiles(7, 10)
    row = jnp.where(me.c == 0, 32 * me.z + 16 * (me.x // 2), 64 * me.x + 16 * (me.z // 2))
    col = jnp.where(me.c == 0, me.x % 2, me.z % 2) * 640
    for dc in range(2):
        for dy in range(2):
            pair = []
            for y in (dy, dy + 2):
                if (y, dc) == (0, 0):
                    pair.append(ysum[me.c, me.ylo].astype(F32))
                else:
                    mirror = ((NY - y) % NY, dc)
                    y_copies[mirror].wait_recv()
                    pair.append(yland[Y_PEERS.index(dict(y=mirror[0], c=mirror[1]))].astype(F32))
            owner = ((me.ylo + dy) % 2) * 2 + (me.c + dc) % 2
            gather[owner, rows_of(row, 16), pl.ds(al(col, 128), 640)] = (pair[0] + pair[1]).astype(BF16)
    later += list(y_copies.values())

    def gather_all(where, order, n, piece, ahead, behind):
        mine = piece(0, 0)
        firsts = [send(mine, mine, as_.at[i], ar.at[i], me.peer(**s)) for i, s in enumerate(where)]
        toward, copies = {1: ahead, -1: behind}, {}
        hops = lambda q, d: n // 2 - (0 if (d == 1) == (q % 2 == 0) else 1)
        for h in range(n // 2):
            for q in order:
                if h == 0 and q:
                    firsts[q - 1].wait_recv()
                for d in (1, -1):
                    if h >= hops(q, d):
                        continue
                    if h:
                        copies[q, d, h - 1].wait_recv()
                    part_of, k = piece(q, -d * h), len(copies)
                    copies[q, d, h] = send(part_of, part_of, bs.at[k], br.at[k], toward[d])
        for q in order:
            for d in (1, -1):
                copies[q, d, hops(q, d) - 1].wait_recv()
        for copy in firsts + list(copies.values()):
            copy.wait_send()

    def owned(row, at):
        return gather.at[:, rows_of(row + 16 * (at // 2), 16), pl.ds(al((at % 2) * 640, 128), 640)]

    @pl.when(me.c == 0)
    def _():
        piece = lambda q, far: owned(32 * ((me.z + far + NZ) % NZ), (me.x - q + NX) % NX)
        gather_all(X_PEERS, (0, 1, 3, 2), NZ, piece, me.peer(z=1), me.peer(z=-1))

    @pl.when(me.c == 1)
    def _():
        piece = lambda q, far: owned(64 * ((me.x + far + NX) % NX), (me.z - q + NZ) % NZ)
        gather_all(Z_PEERS, (0, 1, 7, 2, 6, 3, 5, 4), NX, piece, me.peer(x=1), me.peer(x=-1))

    outs = []
    for s in range(4):
        copy = pltpu.make_async_copy(gather.at[s], gh_ref.at[:, pl.ds(s * WIDE, WIDE)], loc.at[2 + s])
        copy.start()
        outs.append(copy)
    zring.finish()
    xring.finish()
    to_mate.wait_send()
    to_mate_part.wait_send()
    for copy in later + exchanged + crossed + stats + tables + list(hidden.values()) + [grads[i] for i in range(6)]:
        copy.wait_send()
    for copy in outs:
        copy.wait()


def fused(hidden, head_weight, prompt_ids, prompt_counts, sampled_ids, token_mask, rewards):
    vmem = pl.BlockSpec(memory_space=pltpu.VMEM)
    smem = pl.BlockSpec(memory_space=pltpu.SMEM)
    hbm = pl.BlockSpec(memory_space=pl.ANY)
    dma = lambda n: pltpu.SemaphoreType.DMA((n,))
    buf = lambda *shape: pltpu.VMEM(shape, BF16)
    wide = lambda *shape: pltpu.VMEM(shape, F32)
    return pl.pallas_call(
        kernel,
        out_shape=(
            jax.ShapeDtypeStruct((16, 16), F32),
            jax.ShapeDtypeStruct((OWN, 4 * WIDE), BF16),
            jax.ShapeDtypeStruct((WIDE, VOCAB), BF16),
        ),
        in_specs=[hbm, hbm, vmem, vmem, vmem, vmem, smem],
        out_specs=(vmem, hbm, vmem),
        scratch_shapes=[
            buf(WIDE, VOCAB), buf(ALL, WIDE), wide(OWN, VOCAB), wide(OWN, VOCAB), wide(OWN, VOCAB),
            wide(STEPS, STEP, VOCAB), wide(STEPS, STEP, VOCAB), wide(STEPS, STEP, VOCAB), wide(STEPS, STEP, VOCAB),
            wide(16, VOCAB), wide(OWN, 128), wide(OWN, 128), wide(OWN, 128), wide(2, 8, OWN), wide(14, 8, OWN),
            wide(4, 8, OWN), wide(OWN, 128),
            buf(OWN, VOCAB), buf(ALL, VOCAB), wide(4, OWN, WIDE),
            buf(28, 16, 1280), buf(28, 16, 1280), buf(12, 32, 1280), buf(12, 32, 1280),
            buf(2, 32, 1280), buf(2, 64, 1280), buf(3, 2, 16, 640), buf(7, 2, 16, 640), buf(2, 2, 16, 640),
            buf(7, 16, 640), buf(4, OWN, WIDE),
            dma(6), dma(16), dma(16), dma(1), dma(1), dma(1), dma(1), dma(8), dma(8), dma(8), dma(8),
            dma(14), dma(14), dma(10), dma(10), dma(3), dma(3),
            dma(28), dma(28), dma(12), dma(12), dma(3), dma(3), dma(7), dma(7), dma(7), dma(7),
            dma(7), dma(7), dma(28), dma(28),
        ],
        compiler_params=pltpu.CompilerParams(
            collective_id=0, has_side_effects=True, vmem_limit_bytes=56 << 20
        ),
        name="fused",
    )(hidden, head_weight, prompt_ids, prompt_counts, sampled_ids, token_mask, rewards)


def solution(mesh):
    return jax.shard_map(
        fused,
        mesh=mesh,
        in_specs=(
            P("dp", None),
            P("dp", "tensor"),
            P("dp", None),
            P("dp", None),
            P("dp", None),
            P("dp", None),
            P("dp"),
        ),
        out_specs=(P("dp", None), P("dp", None), P("dp", "tensor")),
        check_vma=False,
    )
```

time: 152 us -> 142 us (0.934)
  other arithmetic: 3.48 us -> 0 us
  local copies, waits for them, and re-layouts: 9.06 us -> 6.56 us
  matrix products: 2.25 us -> 0 us
    dot_general x1 -> x0, matrix products: 2.25 us -> none  [penalties(): jnp.einsum('kq,rqv->rkv', earlier, chosen, precision=lax.Precision.HIGHEST)]
    pallas_call x1, Pallas kernels: 136 us -> 135 us  [fused(): pl.pallas_call(kernel, out_shape=(jax.ShapeDtypeStruct((16, 16), F32), ja...]
    unnamed x4 -> x5, local copies, waits for them, and re-layouts: 5.26 us -> 6.56 us
where the time goes in v3:
time: 142 us
  Pallas kernels  135 us (95%)
  local copies, waits for them, and re-layouts  6.56 us (5%)
    pallas_call x1, Pallas kernels, fused(): pl.pallas_call(kernel, out_shape=(jax.ShapeDtypeStruct((16, 16), F32), ja...  135 us
    unnamed x5, local copies, waits for them, and re-layouts  6.56 us

profile of v3, /device:TPU:32, one launch (start us, length us, event | category | flops | bytes accessed | tf_op | source)
XLA Modules:
  0.0 141.7 jit_solution(9936155288478994626)
XLA Ops:
  0.6 134.5 %fused.1 = (f32[16,16]{1,0:T(8,128)}, bf16[256,5120]{1,0:T(8,128)(2,1)}, bf16[1280,1280]{1,0:T(8,128)(2,1)}) custom-call(bf16[256,5120]{1,0:T(8,128)(2,1)} %hid_ref.1, bf16[1280,1280]{1,0:T(8,128)(2,1)} %w_hbm.1, s32[16,32]{1,0:T(8,128)} %pid_ref.1, s32[16,32]{1,0:T(8,128)} %pc_ref.1, s32[16,16]{1,0:T(8,128)} %sid_ref.1, s32[16,16]{1,0:T(8,128)} %mask_ref.1, ...), custom_call_target="tpu_custom_call" | custom-call | tf_op jit(solution)/shard_map/fused/pallas_call | solution.py:475
  135.2 0.0 copy-start
  135.2 1.4 %copy.13 = f32[16,16]{1,0:T(8,128)} copy(f32[16,16]{1,0:T(8,128)} %get-tuple-element.6) | data formatting | bytes 2048
  136.6 3.4 %copy.14 = bf16[256,5120]{1,0:T(8,128)(2,1)} copy(bf16[256,5120]{1,0:T(8,128)(2,1)} %get-tuple-element.7) | data formatting | bytes 5242880
  140.0 0.0 copy-done
  140.0 1.7 %copy.15 = bf16[1280,1280]{1,0:T(8,128)(2,1)} copy(bf16[1280,1280]{1,0:T(8,128)(2,1)S(1)} %copy-done) | data formatting | bytes 6553600
Async XLA Ops:
  135.2 4.9 %copy-start = (bf16[1280,1280]{1,0:T(8,128)(2,1)S(1)}, bf16[1280,1280]{1,0:T(8,128)(2,1)}, u32[]{:S(2)}) copy-start(bf16[1280,1280]{1,0:T(8,128)(2,1)} %get-tuple-element.8) | copy-start | bytes 9830404

commit v4 on v3

v4 whole, which is shorter than its diff:
```python
import functools

import jax
import jax.numpy as jnp
from jax import lax
from jax.experimental import pallas as pl
from jax.experimental.pallas import tpu as pltpu
from jax.sharding import PartitionSpec as P

GROUP = 8
NX, NZ, NY = 4, 8, 4
MESH = pl.DeviceIdType.MESH
F32, BF16 = jnp.float32, jnp.bfloat16

recurrence_deduction = 0.4
presence_deduction = 0.6

class Place:
    def __init__(self):
        dp, t = lax.axis_index("dp"), lax.axis_index("tensor")
        self.ylo, self.c = dp // 2, dp % 2
        self.yhi, self.x, self.z = t // 32, (t // 8) % 4, t % 8
        self.dp = dp

    def peer(self, x=0, y=0, z=0, c=0):
        yy = (self.yhi * 2 + self.ylo + y + NY) % NY
        xx, zz, cc = (self.x + x + NX) % NX, (self.z + z + NZ) % NZ, (self.c + c) % 2
        return ((yy % 2) * 2 + cc, (yy // 2) * 32 + xx * 8 + zz)

    def same_column(self, ylo, yhi, c):
        return (ylo * 2 + c, yhi * 32 + self.x * 8 + self.z)


def arrive(barrier, peers):
    for who in peers:
        pl.semaphore_signal(barrier, inc=1, device_id=who, device_id_type=MESH)


def transfer(src, dst, ssem, rsem, who):
    return pltpu.make_async_remote_copy(
        src_ref=src, dst_ref=dst, send_sem=ssem, recv_sem=rsem, device_id=who, device_id_type=MESH
    )


def send(src, dst, ssem, rsem, who):
    copy = transfer(src, dst, ssem, rsem, who)
    copy.start()
    return copy


Z_PEERS = [dict(z=i) for i in range(1, NZ)]
X_PEERS = [dict(x=i) for i in range(1, NX)]
Y_PEERS = [dict(y=i, c=j) for i in range(NY) for j in range(2) if (i, j) != (0, 0)]
XY_PEERS = [dict(x=i, y=j) for i in range(NX) for j in (0, 2) if (i, j) != (0, 0)]
ALL_PEERS = Z_PEERS + X_PEERS + Y_PEERS + [dict(x=i, y=2) for i in range(1, NX)]

WIDE, VOCAB, OWN, ALL = 1280, 1280, 256, 1024
STEP, STEPS = 32, 8
DIRECT = (1, 3)
EARLY, LATE = 0, 1
PART = 128

def al(i, n):
    return pl.multiple_of(i, n)


def merge(m, l, p, others):
    top = m
    for o in others:
        top = jnp.maximum(top, o[0:1])
    l = l * jnp.exp(m - top)
    for o in others:
        l = l + o[1:2] * jnp.exp(o[0:1] - top)
        p = p + o[2:3]
    return top, l, p


def rows_of(i, n):
    return pl.ds(al(i, n), n)


def kernel(
    hid_ref, w_hbm, pid_ref, pc_ref, sid_ref, mask_ref, rew_ref, lp_ref, gh_ref, gw_ref,
    w_ref, hd, lex, pout, pland, xout, xland, lout, lland, prompt, id_ref, tw_ref, st, mine, sland, tab, cols,
    raw, gr, part, z1land, x1land, s1z, s1x, z2land, x2land, s2, yland, gather,
    loc, hs, hr, cs, cr, ps, pr, xs, xr, ls, lr, ss, sr, gs, grs, ts, tr,
    z1s, z1r, x1s, x1r, z2s, z2r, x2s, x2r, ys, yr, as_, ar, bs, br,
):
    me = Place()
    toward = 1 - 2 * me.ylo
    mate, across, across_mate = me.peer(c=1), me.peer(y=toward), me.peer(y=toward, c=1)
    other = 2 * (1 - me.ylo)
    own, mates = me.dp, 2 * me.ylo + 1 - me.c
    mine_of, mates_of = other + me.c, other + 1 - me.c

    copy_w = pltpu.make_async_copy(w_hbm, w_ref, loc.at[0])
    copy_h = pltpu.make_async_copy(
        hid_ref.at[:, pl.ds(al(own * WIDE, 128), WIDE)], hd.at[rows_of(own * OWN, OWN)], loc.at[1]
    )
    copy_w.start()
    copy_h.start()
    peers = [me.peer(**s) for s in ALL_PEERS]
    barrier = pltpu.get_barrier_semaphore()
    arrive(barrier, peers)

    offset = (me.yhi * 32 + me.x * 8 + me.z) * VOCAB
    column = lax.broadcasted_iota(jnp.int32, (16, VOCAB), 1) + offset
    tile = jnp.zeros((16, VOCAB), F32)
    pid, pc = pid_ref[...], pc_ref[...].astype(F32)
    for j in range(pid.shape[1]):
        tile = tile + jnp.where(pid[:, j : j + 1] == column, pc[:, j : j + 1], 0.0)
    prompt[...] = tile
    diagonal = lax.broadcasted_iota(jnp.int32, (16, 16), 0) == lax.broadcasted_iota(jnp.int32, (16, 16), 1)
    which = lax.broadcasted_iota(jnp.int32, (16, 16), 0)
    advantage = jnp.zeros((16, 16), F32)
    for g in range(16 // GROUP):
        rewards = [rew_ref[g * GROUP + r] for r in range(GROUP)]
        mean = sum(rewards[1:], rewards[0]) * (1.0 / GROUP)
        for r in range(GROUP):
            advantage = jnp.where(which == g * GROUP + r, rewards[r] - mean, advantage)
    weight = -(advantage * mask_ref[...].astype(F32)) * 1.25
    sampled = sid_ref[...].astype(F32)
    for r in range(16):
        at = pl.ds(r * 16, 16)
        for ref, rows in ((id_ref, sampled), (tw_ref, weight)):
            turned = jnp.sum(jnp.where(diagonal, rows[r : r + 1, :], 0.0), axis=1, keepdims=True)
            ref[at, :] = jnp.broadcast_to(turned, (16, 128))
    pl.semaphore_wait(barrier, len(peers))

    def hidden_copy(rel, step, way):
        who = me.peer(y=way, c=rel)
        to = other + (me.c + rel) % 2
        k = rel * STEPS + step
        return pltpu.make_async_remote_copy(
            src_ref=hid_ref.at[rows_of(step * STEP, STEP), pl.ds(al(to * WIDE, 128), WIDE)],
            dst_ref=hd.at[rows_of(own * OWN + step * STEP, STEP)],
            send_sem=hs.at[k],
            recv_sem=hr.at[k],
            device_id=who,
            device_id_type=MESH,
        )

    wrapped = [s for s in range(STEPS) if s not in DIRECT]
    hidden = {}
    for s in range(STEPS):
        for rel in range(2):
            hidden[rel, s] = hidden_copy(rel, s, toward if s in DIRECT else -toward)
    ahead = 2
    for s in (wrapped[0],) + DIRECT[:1]:
        for rel in range(2):
            hidden[rel, s].start()
    to_mate = send(
        hid_ref.at[:, pl.ds(al(mates * WIDE, 128), WIDE)], hd.at[rows_of(own * OWN, OWN)],
        cs.at[0], cr.at[0], mate,
    )
    for s in tuple(wrapped[1:ahead]) + DIRECT[1:]:
        for rel in range(2):
            hidden[rel, s].start()

    copy_w.wait()
    copy_h.wait()
    to_mate.wait_recv()

    @pl.loop(0, 4)
    def _(i):
        at = rows_of(mates * OWN + i * 64, 64)
        pout[rows_of(i * 64, 64)] = jnp.dot(hd[at, :], w_ref[...], preferred_element_type=F32)

    to_mate_part = send(pout, pland, ps.at[0], pr.at[0], mate)
    exchanged, crossed = [], []
    for s in range(STEPS):
        for rel in range(2):
            hidden[rel, s].wait_recv()
        both = jnp.concatenate(
            [hd[rows_of(mates_of * OWN + s * STEP, STEP), :], hd[rows_of(mine_of * OWN + s * STEP, STEP), :]], axis=0
        )
        term = jnp.dot(both, w_ref[...], preferred_element_type=F32)
        xout[s] = term[:STEP]
        exchanged.append(send(xout.at[s], xland.at[s], xs.at[s], xr.at[s], mate))
        if s in wrapped:
            i = wrapped.index(s) + ahead
            if i < len(wrapped):
                for rel in range(2):
                    hidden[rel, wrapped[i]].start()
        exchanged[s].wait_recv()
        lout[s] = term[STEP:] + xland[s]
        crossed.append(send(lout.at[s], lland.at[s], ls.at[s], lr.at[s], across))
        if s == 1:

            @pl.loop(0, 4)
            def _(i):
                lex[rows_of(i * 64, 64)] = jnp.dot(
                    hd[rows_of(own * OWN + i * 64, 64), :], w_ref[...], preferred_element_type=F32
                )

    grads = {}
    lane = lax.broadcasted_iota(jnp.int32, (STEP, 128), 1)
    vocab = (lax.broadcasted_iota(jnp.int32, (STEP, VOCAB), 1) + offset).astype(F32)
    k_of = lax.broadcasted_iota(jnp.int32, (STEP, STEP), 0)
    q_of = lax.broadcasted_iota(jnp.int32, (STEP, STEP), 1)
    earlier = jnp.where((q_of < k_of) & (q_of // 16 == k_of // 16), 1.0, 0.0).astype(BF16)

    def grad_send(k, src, j, lo, n, who):
        grads[k] = send(src, gr.at[rows_of(j * OWN + lo, n)], gs.at[k], grs.at[k], who)

    def local(s):
        crossed[s].wait_recv()
        at = pl.ds(s * STEP, STEP)
        chosen = vocab == id_ref[at, 0:1]
        tally = jnp.dot(earlier, jnp.where(chosen, 1.0, 0.0).astype(BF16), preferred_element_type=F32)
        tally = tally + jnp.concatenate(
            [jnp.broadcast_to(prompt[2 * s + i : 2 * s + i + 1, :], (16, VOCAB)) for i in range(2)], axis=0
        )
        penalty = recurrence_deduction * tally + jnp.where(tally > 0.0, presence_deduction, 0.0)
        scaled = (lex[at, :] + pland[at, :] + lland[s] - penalty) * 1.25
        m = jnp.max(scaled, axis=1, keepdims=True)
        raised = jnp.exp(scaled - m)
        l = jnp.sum(raised, axis=1, keepdims=True)
        p = jnp.sum(jnp.where(chosen, scaled, 0.0), axis=1, keepdims=True)
        raw[at, :] = raised.astype(BF16)
        table = jnp.zeros((STEP, 128), F32)
        for i, v in enumerate((m, l, p, id_ref[at, 0:1], tw_ref[at, 0:1])):
            table = jnp.where(lane == i, v, table)
        st[at, :] = table
        if s % 2:
            lo, n = (s - 1) * STEP, 2 * STEP
            grad_send(s // 2, raw.at[pl.ds(lo, n)], own, lo, n, across)
        if s % 4 == 3:
            lo, n = (s - 3) * STEP, PART
            grad_send(4 + s // 4, raw.at[pl.ds(lo, n)], own, lo, n, mate)

    stats, held, tables = {}, {}, {}

    def stats_send(t, stage, rows):
        mine[t, stage] = rows
        for i, s in enumerate((Z_PEERS, XY_PEERS)[stage]):
            k = (t * 2 + stage) * 7 + i
            stats[k] = send(mine.at[t, stage], sland.at[k], ss.at[k], sr.at[k], me.peer(**s))

    def stats_merge(t, stage, m, l, p):
        ks = [(t * 2 + stage) * 7 + i for i in range(7)]
        for k in ks:
            stats[k].wait_recv()
        return merge(m, l, p, [sland[k] for k in ks])

    def stats_begin(t):
        first = st[pl.ds(t * PART, PART), :].T[0:8]
        held[t] = [first[i : i + 1] for i in range(5)]
        stats_send(t, 0, first)

    def stats_middle(t):
        m, l, p = stats_merge(t, 0, *held[t][:3])
        held[t] += [m, l, p]
        stats_send(t, 1, jnp.concatenate([m, l, p, jnp.zeros((5, PART), F32)], axis=0))

    def stats_end(t):
        own_m, _, _, chosen_id, weight, m, l, p = held[t]
        m, l, p = stats_merge(t, 1, m, l, p)
        norm = m + jnp.log(l)
        logp = p - norm
        lp_ref[pl.ds(t * 8, 8), :] = jnp.concatenate([logp[:, 16 * r : 16 * r + 16] for r in range(8)], axis=0)
        tab[own, t] = jnp.concatenate(
            [weight * jnp.exp(own_m - norm), weight * (1.0 - jnp.exp(logp)), chosen_id, jnp.zeros((5, PART), F32)],
            axis=0,
        )
        for i, who in enumerate((mate, across, across_mate)):
            k = t * 3 + i
            tables[k] = send(tab.at[own, t], tab.at[own, t], ts.at[k], tr.at[k], who)

    def turn(j, t, source, base):
        cols[...] = jnp.concatenate([tab[j, t], jnp.zeros((120, PART), F32)], axis=0).T

        @pl.loop(0, PART // STEP)
        def _(i):
            at, lo = rows_of(i * STEP, STEP), t * PART + i * STEP
            e = source[rows_of(base + lo, STEP), :].astype(F32)
            g = jnp.where(vocab == cols[at, 2:3], cols[at, 1:2], -cols[at, 0:1] * e)
            gr[rows_of(j * OWN + lo, STEP)] = g.astype(BF16)

        part[j, pl.ds(t * PART, PART)] = lax.dot_general(
            gr[rows_of(j * OWN + t * PART, PART), :], w_ref[...], (((1,), (1,)), ((), ())),
            preferred_element_type=F32,
        ).astype(BF16)

    def relay(i):
        grads[i].wait_recv()
        grad_send(6 + i, gr.at[rows_of(mine_of * OWN + i * 64, 64)], mine_of, i * 64, 64, mate)

    def turn_early(t):
        turn(own, t, raw, 0)
        grads[4 + t].wait_recv()
        tables[t * 3].wait_recv()
        turn(mates, t, gr, mates * OWN)

    def turn_late(t):
        for k in (1, 2):
            tables[t * 3 + k].wait_recv()
        for i in (2 * t, 2 * t + 1):
            grads[6 + i].wait_recv()
            grads[6 + i].wait_send()

        @pl.loop(0, 2)
        def _(i):
            turn(other + i, t, gr, (other + i) * OWN)

    one, two, column_y = {}, {}, {}
    ylo_of = {EARLY: me.ylo, LATE: 1 - me.ylo}

    def z_rows(t, half, q):
        return part.at[2 * ylo_of[half], rows_of(t * PART + 16 * q, 16)]

    def x_rows(t, half, q):
        return part.at[2 * ylo_of[half] + 1, rows_of(t * PART + 32 * q, 32)]

    def one_send(t, half):
        for i in (4, 3, 5, 2, 6, 1, 7):
            k = (t * 2 + half) * 7 + i - 1
            one["z", k] = send(
                z_rows(t, half, (me.z + i) % NZ), z1land.at[k], z1s.at[k], z1r.at[k], me.peer(z=i)
            )
        for i in (2, 1, 3):
            k = (t * 2 + half) * 3 + i - 1
            one["x", k] = send(
                x_rows(t, half, (me.x + i) % NX), x1land.at[k], x1s.at[k], x1r.at[k], me.peer(x=i)
            )

    def one_total(axis, t, half):
        n, land = (7, z1land) if axis == "z" else (3, x1land)
        term = (z_rows(t, half, me.z) if axis == "z" else x_rows(t, half, me.x))[...].astype(F32)
        for i in range(n):
            k = (t * 2 + half) * n + i
            one[axis, k].wait_recv()
            term = term + land[k].astype(F32)
        return term.astype(BF16)

    def half_cols(i):
        return pl.ds(al((i % 2) * 640, 128), 640)

    def z_cut(t, x):
        return s1z.at[t, x // 2, :, half_cols(x)]

    def x_cut(t, z):
        return s1x.at[t, (z // 2) % 2, rows_of((z // 4) * 16, 16), half_cols(z)]

    def two_send_x(t):
        for half in (EARLY, LATE):
            s1x[t, ylo_of[half]] = one_total("x", t, half)
        for i in (4, 3, 5, 2, 6, 1, 7):
            k = t * 7 + i - 1
            two["x", k] = send(x_cut(t, (me.z + i) % NZ), x2land.at[k], x2s.at[k], x2r.at[k], me.peer(z=i))

    def two_send_z(t):
        for half in (EARLY, LATE):
            s1z[t, ylo_of[half]] = one_total("z", t, half)
        for i in (2, 1, 3):
            k = t * 3 + i - 1
            two["z", k] = send(z_cut(t, (me.x + i) % NX), z2land.at[k], z2s.at[k], z2r.at[k], me.peer(x=i))

    slot = (me.yhi * 2 + me.ylo) * 2 + me.c
    kept_by = (me.x // 2, (me.z // 2) % 2)
    keeps = ((me.c == 0) & (kept_by[0] == me.ylo)) | ((me.c == 1) & (kept_by[1] == me.ylo))

    def y_copy(t, core, yhi):
        k = t * 4 + core * 2 + yhi
        to = me.same_column(kept_by[core], yhi, core)
        return transfer(s2.at[t, core], yland.at[t, slot], ys.at[k], yr.at[t * 8 + slot], to)

    def y_each(t, act):
        for core in range(2):
            for yhi in range(2):

                @pl.when((me.c != core) | (me.ylo != kept_by[core]) | (me.yhi != yhi))
                def _():
                    act(y_copy(t, core, yhi))

    def y_send(t):
        for core, (axis, ours, land, n) in enumerate(
            (("z", z_cut(t, me.x), z2land, 3), ("x", x_cut(t, me.z), x2land, 7))
        ):
            term = ours[...].astype(F32)
            for i in range(n):
                k = t * n + i
                two[axis, k].wait_recv()
                term = term + land[k].astype(F32)
            s2[t, core] = term.astype(BF16)
        y_each(t, lambda copy: copy.start())

        @pl.when(keeps)
        def _():
            yland[t, slot] = s2[t, me.c]

    def piece(t, x, z):
        row = jnp.where(me.c == 0, 16 * z, 32 * x + 16 * (z // 4))
        col = jnp.where(me.c == 0, x % 2, z % 2) * 640
        return gather.at[:, rows_of(t * PART + row, 16), pl.ds(al(col, 128), 640)]

    def first_out(t, core, i):
        at, k = piece(t, me.x, me.z), t * 7 + i - 1
        return transfer(at, at, as_.at[k], ar.at[k], me.peer(x=i) if core == 0 else me.peer(z=i))

    def first_in(t, core, i):
        x, z = ((me.x - i + NX) % NX, me.z) if core == 0 else (me.x, (me.z - i + NZ) % NZ)
        at, k = piece(t, x, z), t * 7 + i - 1
        return transfer(at, at, as_.at[k], ar.at[k], me.peer(x=-i) if core == 0 else me.peer(z=-i))

    def y_take(t):
        @pl.when(keeps)
        def _():
            for k in range(8):

                @pl.when(k != slot)
                def _():
                    transfer(
                        s2.at[t, 0], yland.at[t, k], ys.at[t * 4], yr.at[t * 8 + k], mate
                    ).wait_recv()

            mine_at = piece(t, me.x, me.z)
            for s in range(4):
                k = (s // 2) * 2 + s % 2
                pair = yland[t, k].astype(F32) + yland[t, k + 4].astype(F32)
                mine_at.at[s][...] = pair.astype(BF16)

            for core in range(2):

                @pl.when(me.c == core)
                def _():
                    for i in ((2, 1, 3), (4, 3, 5, 2, 6, 1, 7))[core]:
                        first_out(t, core, i).start()

    def z_rows_of(t, z, halves=None):
        at = gather.at[:, rows_of(t * PART + 16 * ((z + NZ) % NZ), 16)]
        return at if halves is None else at.at[:, :, pl.ds(halves * 640, 640)]

    def x_rows_of(t, x):
        return gather.at[:, rows_of(t * PART + 32 * ((x + NX) % NX), 32)]

    Z_STEPS = [(2, 2, None), (-2, -2, None), (1, 1, None), (-1, -1, None), (1, 3, None), (-1, -3, None), (2, 4, 0), (-2, -4, 1)]

    def z_out(t, k):
        away, origin, halves = Z_STEPS[k]
        at = z_rows_of(t, me.z - (origin - away), halves)
        return transfer(at, at, bs.at[t * 8 + k], br.at[t * 8 + k], me.peer(z=away))

    def z_in(t, k):
        away, origin, halves = Z_STEPS[k]
        at = z_rows_of(t, me.z - origin, halves)
        return transfer(at, at, bs.at[t * 8 + k], br.at[t * 8 + k], me.peer(z=-away))

    X_STEPS = [2, 1, -1]

    def x_out(t, k):
        at = x_rows_of(t, me.x)
        return transfer(at, at, bs.at[t * 8 + k], br.at[t * 8 + k], me.peer(x=X_STEPS[k]))

    def x_in(t, k):
        at = x_rows_of(t, me.x - X_STEPS[k])
        return transfer(at, at, bs.at[t * 8 + k], br.at[t * 8 + k], me.peer(x=-X_STEPS[k]))

    def gather_begin(t):
        for core in range(2):

            @pl.when(me.c == core)
            def _():
                for i in ((1, 3, 2), (1, 7, 2, 6, 3, 5, 4))[core]:
                    far = (me.x - i + NX) % NX // 2 if core == 0 else (me.z - i + NZ) % NZ // 2 % 2

                    @pl.when(far == me.ylo)
                    def _():
                        first_in(t, core, i).wait_recv()

                for k in range(4 if core == 0 else 3):
                    (z_out if core == 0 else x_out)(t, k).start()

    def gather_middle(t):
        @pl.when(me.c == 0)
        def _():
            z_in(t, 0).wait_recv()
            z_out(t, 4).start()
            z_out(t, 6).start()
            z_in(t, 1).wait_recv()
            z_out(t, 5).start()
            z_out(t, 7).start()

    def gather_end(t):
        @pl.when(me.c == 0)
        def _():
            for k in range(2, 8):
                z_in(t, k).wait_recv()

        @pl.when(me.c == 1)
        def _():
            for k in range(3):
                x_in(t, k).wait_recv()

        for s in range(4):
            out_copy(t, s).start()

    def out_copy(t, s):
        at = pl.ds(t * PART, PART)
        return pltpu.make_async_copy(
            gather.at[s, at], gh_ref.at[at, pl.ds(s * WIDE, WIDE)], loc.at[2 + t * 4 + s]
        )

    def gather_drain(t):
        @pl.when(keeps)
        def _():
            for core in range(2):

                @pl.when(me.c == core)
                def _():
                    for i in range(1, NX if core == 0 else NZ):
                        first_out(t, core, i).wait_send()

        @pl.when(me.c == 0)
        def _():
            for k in range(8):
                z_out(t, k).wait_send()

        @pl.when(me.c == 1)
        def _():
            for k in range(3):
                x_out(t, k).wait_send()

    def weight_tiles(lo, hi):
        @pl.loop(lo, hi)
        def _(i):
            at = pl.ds(al(i * 128, 128), 128)
            gw_ref[at, :] = lax.dot_general(
                hd[:, at], gr[...], (((0,), (0,)), ((), ())), preferred_element_type=F32
            ).astype(BF16)

    to_mate_part.wait_recv()
    for s in range(4):
        local(s)
    stats_begin(0)
    local(4)
    local(5)
    stats_middle(0)
    local(6)
    stats_end(0)
    local(7)
    stats_begin(1)
    turn_early(0)
    one_send(0, EARLY)
    relay(0)
    stats_middle(1)
    relay(1)
    turn_late(0)
    one_send(0, LATE)
    stats_end(1)
    relay(2)
    turn_early(1)
    one_send(1, EARLY)
    two_send_x(0)
    relay(3)
    turn_late(1)
    one_send(1, LATE)
    two_send_z(0)
    weight_tiles(0, 2)
    y_send(0)
    weight_tiles(2, 3)
    two_send_x(1)
    y_take(0)
    weight_tiles(3, 4)
    two_send_z(1)
    gather_begin(0)
    weight_tiles(4, 6)
    y_send(1)
    gather_middle(0)
    weight_tiles(6, 8)
    y_take(1)
    weight_tiles(8, 10)
    gather_begin(1)
    gather_end(0)
    gather_middle(1)
    to_mate.wait_send()
    to_mate_part.wait_send()
    for copy in (
        exchanged + crossed + list(hidden.values()) + [grads[i] for i in range(6)] + list(stats.values())
        + list(tables.values()) + list(one.values()) + list(two.values())
    ):
        copy.wait_send()
    for t in range(2):
        y_each(t, lambda copy: copy.wait_send())
    gather_end(1)
    for t in range(2):
        gather_drain(t)
    for t in range(2):
        for s in range(4):
            out_copy(t, s).wait()


def fused(hidden, head_weight, prompt_ids, prompt_counts, sampled_ids, token_mask, rewards):
    vmem = pl.BlockSpec(memory_space=pltpu.VMEM)
    smem = pl.BlockSpec(memory_space=pltpu.SMEM)
    hbm = pl.BlockSpec(memory_space=pl.ANY)
    dma = lambda n: pltpu.SemaphoreType.DMA((n,))
    buf = lambda *shape: pltpu.VMEM(shape, BF16)
    wide = lambda *shape: pltpu.VMEM(shape, F32)
    return pl.pallas_call(
        kernel,
        out_shape=(
            jax.ShapeDtypeStruct((16, 16), F32),
            jax.ShapeDtypeStruct((OWN, 4 * WIDE), BF16),
            jax.ShapeDtypeStruct((WIDE, VOCAB), BF16),
        ),
        in_specs=[hbm, hbm, vmem, vmem, vmem, vmem, smem],
        out_specs=(vmem, hbm, vmem),
        scratch_shapes=[
            buf(WIDE, VOCAB), buf(ALL, WIDE), wide(OWN, VOCAB), wide(OWN, VOCAB), wide(OWN, VOCAB),
            wide(STEPS, STEP, VOCAB), wide(STEPS, STEP, VOCAB), wide(STEPS, STEP, VOCAB), wide(STEPS, STEP, VOCAB),
            wide(16, VOCAB), wide(OWN, 128), wide(OWN, 128), wide(OWN, 128), wide(2, 2, 8, PART), wide(28, 8, PART),
            wide(4, 2, 8, PART), wide(PART, 128),
            buf(OWN, VOCAB), buf(ALL, VOCAB), buf(4, OWN, WIDE),
            buf(28, 16, WIDE), buf(12, 32, WIDE), buf(2, 2, 16, WIDE), buf(2, 2, 32, WIDE),
            buf(6, 16, 640), buf(14, 16, 640), buf(2, 2, 16, 640), buf(2, 8, 16, 640), buf(4, OWN, WIDE),
            dma(10), dma(16), dma(16), dma(1), dma(1), dma(1), dma(1), dma(8), dma(8), dma(8), dma(8),
            dma(28), dma(28), dma(10), dma(10), dma(6), dma(6),
            dma(28), dma(28), dma(12), dma(12), dma(6), dma(6), dma(14), dma(14), dma(8), dma(16),
            dma(14), dma(14), dma(16), dma(16),
        ],
        compiler_params=pltpu.CompilerParams(
            collective_id=0, has_side_effects=True, vmem_limit_bytes=56 << 20
        ),
        name="fused",
    )(hidden, head_weight, prompt_ids, prompt_counts, sampled_ids, token_mask, rewards)


def solution(mesh):
    return jax.shard_map(
        fused,
        mesh=mesh,
        in_specs=(
            P("dp", None),
            P("dp", "tensor"),
            P("dp", None),
            P("dp", None),
            P("dp", None),
            P("dp", None),
            P("dp"),
        ),
        out_specs=(P("dp", None), P("dp", None), P("dp", "tensor")),
        check_vma=False,
    )
```

time: 142 us -> 146 us (1.028)
  Pallas kernels: 135 us -> 137 us
    pallas_call x1, Pallas kernels: 135 us -> 137 us  [fused(): pl.pallas_call(kernel, out_shape=(jax.ShapeDtypeStruct((16, 16), F32), ja...]
where the time goes in v4:
time: 146 us; the launch traced here: 144 us
  Pallas kernels  137 us (94%)
  local copies, waits for them, and re-layouts  6.56 us (4%)
    pallas_call x1, Pallas kernels, fused(): pl.pallas_call(kernel, out_shape=(jax.ShapeDtypeStruct((16, 16), F32), ja...  137 us
    unnamed x5, local copies, waits for them, and re-layouts  6.56 us

profile of v4, /device:TPU:32, one launch (start us, length us, event | category | flops | bytes accessed | tf_op | source)
XLA Modules:
  0.0 144.3 jit_solution(16043564942227507813)
XLA Ops:
  0.6 137.1 %fused.1 = (f32[16,16]{1,0:T(8,128)}, bf16[256,5120]{1,0:T(8,128)(2,1)}, bf16[1280,1280]{1,0:T(8,128)(2,1)}) custom-call(bf16[256,5120]{1,0:T(8,128)(2,1)} %hid_ref.1, bf16[1280,1280]{1,0:T(8,128)(2,1)} %w_hbm.1, s32[16,32]{1,0:T(8,128)} %pid_ref.1, s32[16,32]{1,0:T(8,128)} %pc_ref.1, s32[16,16]{1,0:T(8,128)} %sid_ref.1, s32[16,16]{1,0:T(8,128)} %mask_ref.1, ...), custom_call_target="tpu_custom_call" | custom-call | tf_op jit(solution)/shard_map/fused/pallas_call | solution.py:600
  137.8 0.0 copy-start
  137.8 1.4 %copy.13 = f32[16,16]{1,0:T(8,128)} copy(f32[16,16]{1,0:T(8,128)} %get-tuple-element.6) | data formatting | bytes 2048
  139.2 3.4 %copy.14 = bf16[256,5120]{1,0:T(8,128)(2,1)} copy(bf16[256,5120]{1,0:T(8,128)(2,1)} %get-tuple-element.7) | data formatting | bytes 5242880
  142.6 0.0 copy-done
  142.6 1.7 %copy.15 = bf16[1280,1280]{1,0:T(8,128)(2,1)} copy(bf16[1280,1280]{1,0:T(8,128)(2,1)S(1)} %copy-done) | data formatting | bytes 6553600
Async XLA Ops:
  137.8 4.9 %copy-start = (bf16[1280,1280]{1,0:T(8,128)(2,1)S(1)}, bf16[1280,1280]{1,0:T(8,128)(2,1)}, u32[]{:S(2)}) copy-start(bf16[1280,1280]{1,0:T(8,128)(2,1)} %get-tuple-element.8) | copy-start | bytes 9830404

commit v5 on v3

--- a/solution.py
+++ b/solution.py
@@ -51,6 +51,7 @@
 STEP, STEPS = 32, 8
 DIRECT = (1, 3)
 EARLY, LATE = 0, 1
+PART = 128
 CHAINS = [(d, half, sub, (d == 1) == (sub == 0)) for half in (EARLY, LATE) for sub in range(2) for d in (1, -1)]
 
 
@@ -70,9 +71,9 @@
     def hops(self, i):
         return self.n // 2 - (0 if CHAINS[i][3] else 1)
 
-    def step(self, half, h):
-        for i, (d, hf, sub, far) in enumerate(CHAINS):
-            if h >= self.hops(i) or hf != half:
+    def step(self, half, sub, h):
+        for i, (d, hf, sb, far) in enumerate(CHAINS):
+            if h >= self.hops(i) or (hf, sb) != (half, sub):
                 continue
             chunk = (self.at + d * (self.hops(i) - h) + self.n) % self.n
             term = self.get(half, sub, chunk)
@@ -115,9 +116,9 @@
 
 def kernel(
     hid_ref, w_hbm, pid_ref, pc_ref, sid_ref, mask_ref, rew_ref, lp_ref, gh_ref, gw_ref,
-    w_ref, hd, lex, pout, pland, xout, xland, lout, lland, prompt, id_ref, tw_ref, st, mine, sland, tab, cols,
-    raw, gr, part, zout, zland, xrout, xrland, z2, x2, z2land, x2land, ysum, yland, gather,
-    loc, hs, hr, cs, cr, ps, pr, xs, xr, ls, lr, ss, sr, gs, grs, ts, tr,
+    w_ref, wt_ref, hd, lex, pout, pland, xout, xland, lout, lland, prompt, sids, id_ref, tw_ref, st, mine, sland, tab, cols,
+    raw, gr, part, plain, gw_tiles, zout, zland, xrout, xrland, z2, x2, z2land, x2land, ysum, yland, gather,
+    loc, is_, ir, hs, hr, cs, cr, ps, pr, xs, xr, ls, lr, ss, sr, gs, grs, ts, tr,
     zs, zr, xrs, xrr, z2s, z2r, x2s, x2r, ys, yr, as_, ar, bs, br,
 ):
     me = Place()
@@ -144,7 +145,12 @@
     for j in range(pid.shape[1]):
         tile = tile + jnp.where(pid[:, j : j + 1] == column, pc[:, j : j + 1], 0.0)
     prompt[...] = tile
-    diagonal = lax.broadcasted_iota(jnp.int32, (16, 16), 0) == lax.broadcasted_iota(jnp.int32, (16, 16), 1)
+    its_lane = lax.broadcasted_iota(jnp.int32, (OWN, 16), 1) == lax.broadcasted_iota(jnp.int32, (OWN, 16), 0) % 16
+
+    def as_column(rows):
+        wide_rows = jnp.concatenate([jnp.broadcast_to(rows[r : r + 1, :], (16, 16)) for r in range(16)], axis=0)
+        return jnp.broadcast_to(jnp.sum(jnp.where(its_lane, wide_rows, 0.0), axis=1, keepdims=True), (OWN, 128))
+
     which = lax.broadcasted_iota(jnp.int32, (16, 16), 0)
     advantage = jnp.zeros((16, 16), F32)
     for g in range(16 // GROUP):
@@ -153,12 +159,9 @@
         for r in range(GROUP):
             advantage = jnp.where(which == g * GROUP + r, rewards[r] - mean, advantage)
     weight = -(advantage * mask_ref[...].astype(F32)) * 1.25
-    sampled = sid_ref[...].astype(F32)
-    for r in range(16):
-        at = pl.ds(r * 16, 16)
-        for ref, rows in ((id_ref, sampled), (tw_ref, weight)):
-            turned = jnp.sum(jnp.where(diagonal, rows[r : r + 1, :], 0.0), axis=1, keepdims=True)
-            ref[at, :] = jnp.broadcast_to(turned, (16, 128))
+    sids[own] = sid_ref[...]
+    id_ref[rows_of(own * OWN, OWN)] = as_column(sid_ref[...].astype(F32))
+    tw_ref[...] = as_column(weight)
     pl.semaphore_wait(barrier, len(peers))
 
     def hidden_copy(rel, step, way):
@@ -191,7 +194,16 @@
         for rel in range(2):
             hidden[rel, s].start()
 
+    id_copies = [
+        send(sids.at[own], sids.at[own], is_.at[i], ir.at[i], who) for i, who in enumerate((mate, across, across_mate))
+    ]
     copy_w.wait()
+
+    @pl.loop(0, 10)
+    def _(i):
+        at = pl.ds(al(i * 128, 128), 128)
+        wt_ref[:, at] = w_ref[at, :].T
+
     copy_h.wait()
     to_mate.wait_recv()
 
@@ -202,6 +214,15 @@
 
     to_mate_part = send(pout, pland, ps.at[0], pr.at[0], mate)
     exchanged, crossed = [], []
+    vocab = (lax.broadcasted_iota(jnp.int32, (STEP, VOCAB), 1) + offset).astype(F32)
+    vocab_wide = (lax.broadcasted_iota(jnp.int32, (64, VOCAB), 1) + offset).astype(F32)
+
+    def sampled_rows(j):
+        @pl.loop(0, 4)
+        def _(i):
+            chosen = jnp.where(vocab_wide == id_ref[rows_of(j * OWN + i * 64, 64), 0:1], 1.0, 0.0)
+            part[j, rows_of(i * 64, 64)] = jnp.dot(chosen.astype(BF16), wt_ref[...], preferred_element_type=F32)
+
     for s in range(STEPS):
         for rel in range(2):
             hidden[rel, s].wait_recv()
@@ -227,6 +248,15 @@
                     hd[rows_of(own * OWN + i * 64, 64), :], w_ref[...], preferred_element_type=F32
                 )
 
+        if s == 2:
+            for copy in id_copies:
+                copy.wait_recv()
+            for i in range(1, 4):
+                j = (own + i) % 4
+                id_ref[rows_of(j * OWN, OWN)] = as_column(sids[j].astype(F32))
+        if 3 <= s < 7:
+            sampled_rows(s - 3)
+
     grads = {}
 
     def grad_send(k, src, j, lo, n, who):
@@ -234,14 +264,14 @@
 
     to_mate_part.wait_recv()
     lane = lax.broadcasted_iota(jnp.int32, (STEP, 128), 1)
-    vocab = (lax.broadcasted_iota(jnp.int32, (STEP, VOCAB), 1) + offset).astype(F32)
     k_of = lax.broadcasted_iota(jnp.int32, (STEP, STEP), 0)
     q_of = lax.broadcasted_iota(jnp.int32, (STEP, STEP), 1)
     earlier = jnp.where((q_of < k_of) & (q_of // 16 == k_of // 16), 1.0, 0.0).astype(BF16)
     for s in range(STEPS):
         crossed[s].wait_recv()
         at = pl.ds(s * STEP, STEP)
-        chosen = vocab == id_ref[at, 0:1]
+        ids = id_ref[rows_of(own * OWN + s * STEP, STEP), 0:1]
+        chosen = vocab == ids
         tally = jnp.dot(earlier, jnp.where(chosen, 1.0, 0.0).astype(BF16), preferred_element_type=F32)
         tally = tally + jnp.concatenate(
             [jnp.broadcast_to(prompt[2 * s + i : 2 * s + i + 1, :], (16, VOCAB)) for i in range(2)], axis=0
@@ -252,9 +282,9 @@
         raised = jnp.exp(scaled - m)
         l = jnp.sum(raised, axis=1, keepdims=True)
         p = jnp.sum(jnp.where(chosen, scaled, 0.0), axis=1, keepdims=True)
-        raw[at, :] = raised.astype(BF16)
+        raw[at, :] = jnp.where(chosen, 0.0, raised).astype(BF16)
         table = jnp.zeros((STEP, 128), F32)
-        for i, v in enumerate((m, l, p, id_ref[at, 0:1], tw_ref[at, 0:1])):
+        for i, v in enumerate((m, l, p, tw_ref[at, 0:1])):
             table = jnp.where(lane == i, v, table)
         st[at, :] = table
         if s % 2:
@@ -264,15 +294,34 @@
             lo, n = (s - 3) * STEP, 4 * STEP
             grad_send(4 + s // 4, raw.at[pl.ds(lo, n)], own, lo, n, mate)
     first = st[...].T[0:8]
-    m, l, p, chosen_id, weight = [first[i : i + 1] for i in range(5)]
+    m, l, p, weight = [first[i : i + 1] for i in range(4)]
     own_m, across_rows = m, first
     stats = []
+
+    def product(j, lo, n, src, base):
+        plain[rows_of(j * OWN + lo, n)] = jnp.dot(
+            src[rows_of(base + lo, n), :], wt_ref[...], preferred_element_type=F32
+        )
+
+    def relay(i):
+        grads[i].wait_recv()
+        grad_send(6 + i, gr.at[rows_of(mine_of * OWN + i * 64, 64)], mine_of, i * 64, 64, mate)
+
     for stage, where in enumerate((Z_PEERS, XY_PEERS)):
         mine[stage] = across_rows
         copies = []
         for i, s in enumerate(where):
             k = stage * 7 + i
             copies.append(send(mine.at[stage], sland.at[k], ss.at[k], sr.at[k], me.peer(**s)))
+        if stage == 0:
+            product(own, 0, OWN, raw, 0)
+        else:
+            grads[4].wait_recv()
+            grads[5].wait_recv()
+            product(mates, 0, OWN, gr, mates * OWN)
+            relay(0)
+            relay(1)
+            product(mine_of, 0, PART, gr, mine_of * OWN)
         for copy in copies:
             copy.wait_recv()
         stats += copies
@@ -283,86 +332,99 @@
     lp_ref[...] = jnp.concatenate([logp[:, 16 * r : 16 * r + 16] for r in range(16)], axis=0)
 
     tab[own] = jnp.concatenate(
-        [weight * jnp.exp(own_m - norm), weight * (1.0 - jnp.exp(logp)), chosen_id, jnp.zeros((5, OWN), F32)], axis=0
+        [weight * jnp.exp(own_m - norm), weight * (1.0 - jnp.exp(logp)), jnp.zeros((6, OWN), F32)], axis=0
     )
     tables = [send(tab.at[own], tab.at[own], ts.at[i], tr.at[i], who) for i, who in enumerate((mate, across, across_mate))]
 
-    def turn(j, src, base):
-        wide_rows = jnp.concatenate([tab[j], jnp.zeros((120, OWN), F32)], axis=0)
-        cols[...] = wide_rows.T
-
-        @pl.loop(0, OWN // STEP)
+    def scale(j, t):
+        table, at_j = tab[j][:, t * PART : (t + 1) * PART], rows_of(j * OWN + t * PART, PART)
+        cols[at_j] = jnp.concatenate([table, jnp.zeros((120, PART), F32)], axis=0).T
+
+        @pl.loop(0, PART // STEP)
         def _(i):
-            at, to = rows_of(i * STEP, STEP), rows_of(j * OWN + i * STEP, STEP)
-            g = jnp.where(
-                vocab == cols[at, 2:3], cols[at, 1:2], -cols[at, 0:1] * src[rows_of(base + i * STEP, STEP), :].astype(F32)
-            )
-            gr[to, :] = g.astype(BF16)
-
-        part[j] = lax.dot_general(
-            gr[rows_of(j * OWN, OWN), :], w_ref[...], (((1,), (1,)), ((), ())), preferred_element_type=F32
-        )
-
-    def relay(i):
-        grads[i].wait_recv()
-        grad_send(6 + i, gr.at[rows_of(mine_of * OWN + i * 64, 64)], mine_of, i * 64, 64, mate)
+            lo = t * PART + i * STEP
+            at, to = rows_of(lo, STEP), rows_of(j * OWN + lo, STEP)
+            part[j, at] = cols[to, 1:2] * part[j, at] - cols[to, 0:1] * plain[to, :]
+
+    def turn(lo, hi):
+        @pl.loop(lo, hi)
+        def _(i):
+            at = rows_of(i * STEP, STEP)
+            g = jnp.where(vocab == id_ref[at, 0:1], cols[at, 1:2], -cols[at, 0:1] * gr[at, :].astype(F32))
+            gr[at] = g.astype(BF16)
 
     def z_get(half, sub, chunk):
         ylo = me.ylo if half == EARLY else 1 - me.ylo
-        return part[2 * ylo, rows_of(chunk * 32 + sub * 16, 16), :]
+        return part[2 * ylo, rows_of(sub * PART + chunk * 16, 16), :]
 
     def x_get(half, sub, chunk):
         ylo = me.ylo if half == EARLY else 1 - me.ylo
-        return part[2 * ylo + 1, rows_of(chunk * 64 + sub * 32, 32), :]
+        return part[2 * ylo + 1, rows_of(sub * PART + chunk * 32, 32), :]
 
     zring = Ring(NZ, me.z, z_get, zout, zland, zs, zr, me.peer(z=1), me.peer(z=-1))
     xring = Ring(NX, me.x, x_get, xrout, xrland, xrs, xrr, me.peer(x=1), me.peer(x=-1))
-    relay(0)
-    relay(1)
-    turn(own, raw, 0)
-    grads[4].wait_recv()
-    grads[5].wait_recv()
+    def begin(half, t):
+        zring.step(half, t, 0)
+        xring.step(half, t, 0)
+
+    def late(t):
+        if t == 0:
+            tables[1].wait_recv()
+            tables[2].wait_recv()
+        for i in (2 * t, 2 * t + 1):
+            grads[6 + i].wait_recv()
+        product(mates_of, t * PART, PART, gr, mates_of * OWN)
+
+        @pl.loop(0, 2)
+        def _(i):
+            scale(other + i, t)
+
+        begin(LATE, t)
+
+    scale(own, 0)
+    scale(own, 1)
     tables[0].wait_recv()
-    turn(mates, gr, mates * OWN)
-    zring.step(EARLY, 0)
-    xring.step(EARLY, 0)
+    scale(mates, 0)
+    scale(mates, 1)
+    begin(EARLY, 0)
+    begin(EARLY, 1)
+    late(0)
     relay(2)
-    zring.step(EARLY, 1)
     relay(3)
-    xring.step(EARLY, 1)
-    for copy in tables[1:]:
-        copy.wait_recv()
-    for i in range(4):
-        grads[6 + i].wait_recv()
-        grads[6 + i].wait_send()
-
-    @pl.loop(0, 2)
-    def _(i):
-        turn(other + i, gr, (other + i) * OWN)
+    product(mine_of, PART, PART, gr, mine_of * OWN)
+    zring.step(EARLY, 0, 1)
+    xring.step(EARLY, 0, 1)
+    late(1)
+    zring.step(EARLY, 1, 1)
+    xring.step(EARLY, 1, 1)
+    zring.step(LATE, 0, 1)
+    xring.step(LATE, 0, 1)
+    zring.step(EARLY, 0, 2)
+    zring.step(EARLY, 1, 2)
+    zring.step(LATE, 1, 1)
+    xring.step(LATE, 1, 1)
+    zring.step(LATE, 0, 2)
+    zring.step(EARLY, 0, 3)
+    zring.step(EARLY, 1, 3)
+    for i in range(6, 10):
+        grads[i].wait_send()
+    own_at = rows_of(own * OWN, OWN)
+    gr[own_at] = raw[...]
 
     def weight_tiles(lo, hi):
         @pl.loop(lo, hi)
         def _(i):
             at = pl.ds(al(i * 128, 128), 128)
-            gw_ref[at, :] = lax.dot_general(
+            gw_tiles[at, :] = lax.dot_general(
                 hd[:, at], gr[...], (((0,), (0,)), ((), ())), preferred_element_type=F32
             ).astype(BF16)
-
-    zring.step(LATE, 0)
-    xring.step(LATE, 0)
-    zring.step(EARLY, 2)
-    weight_tiles(0, 1)
-    zring.step(LATE, 1)
-    xring.step(LATE, 1)
-    zring.step(EARLY, 3)
-    weight_tiles(1, 2)
 
     def cut(ref, at):
         rows = rows_of((at // 2) * 16, 16)
         return ref.at[:, rows, pl.ds(al((at % 2) * 640, 128), 640)]
 
     later = []
-    zring.step(LATE, 2)
+    zring.step(LATE, 1, 2)
     for half, ylo in ((EARLY, me.ylo), (LATE, 1 - me.ylo)):
         for sub in range(2):
             x2[ylo, pl.ds(sub * 32, 32)] = xring.total(half, sub).astype(BF16)
@@ -371,9 +433,11 @@
         x_copies.append(
             send(cut(x2, (me.z + i) % NZ), x2land.at[i - 1], x2s.at[i - 1], x2r.at[i - 1], me.peer(z=i))
         )
-    weight_tiles(2, 3)
-    zring.step(LATE, 3)
-    weight_tiles(3, 5)
+    zring.step(LATE, 0, 3)
+    turn(0, 16)
+    zring.step(LATE, 1, 3)
+    turn(16, 32)
+    weight_tiles(0, 2)
     for half, ylo in ((EARLY, me.ylo), (LATE, 1 - me.ylo)):
         for sub in range(2):
             z2[ylo, pl.ds(sub * 16, 16)] = zring.total(half, sub).astype(BF16)
@@ -382,7 +446,7 @@
         z_copies.append(
             send(cut(z2, (me.x + i) % NX), z2land.at[i - 1], z2s.at[i - 1], z2r.at[i - 1], me.peer(x=i))
         )
-    weight_tiles(5, 7)
+    weight_tiles(2, 6)
     for core, (ours, land, copies) in enumerate(
         ((cut(z2, me.x), z2land, z_copies), (cut(x2, me.z), x2land, x_copies))
     ):
@@ -394,13 +458,22 @@
         ysum[core] = term.astype(BF16)
         later += copies
 
+    def kept_rows(core, x, z):
+        return 16 * z + PART * (x // 2) if core == 0 else 32 * x + PART * (z // 4) + 16 * ((z // 2) % 2)
+
+    def kept_cols(core, x, z):
+        return (x % 2 if core == 0 else z % 2) * 640
+
     y_copies = {}
     for i, s in enumerate(Y_PEERS):
         piece = ysum.at[(me.c + s["c"]) % 2, (me.ylo + s["y"]) % 2]
         y_copies[s["y"], s["c"]] = send(piece, yland.at[i], ys.at[i], yr.at[i], me.peer(**s))
-    weight_tiles(7, 10)
-    row = jnp.where(me.c == 0, 32 * me.z + 16 * (me.x // 2), 64 * me.x + 16 * (me.z // 2))
-    col = jnp.where(me.c == 0, me.x % 2, me.z % 2) * 640
+    weight_tiles(6, 10)
+    gw_out = pltpu.make_async_copy(gw_tiles, gw_ref, loc.at[6])
+    gw_out.start()
+    row, col = kept_rows(0, me.x, me.z), kept_cols(0, me.x, me.z)
+    row = jnp.where(me.c == 0, row, kept_rows(1, me.x, me.z))
+    col = jnp.where(me.c == 0, col, kept_cols(1, me.x, me.z))
     for dc in range(2):
         for dy in range(2):
             pair = []
@@ -415,40 +488,85 @@
             gather[owner, rows_of(row, 16), pl.ds(al(col, 128), 640)] = (pair[0] + pair[1]).astype(BF16)
     later += list(y_copies.values())
 
-    def gather_all(where, order, n, piece, ahead, behind):
-        mine = piece(0, 0)
-        firsts = [send(mine, mine, as_.at[i], ar.at[i], me.peer(**s)) for i, s in enumerate(where)]
-        toward, copies = {1: ahead, -1: behind}, {}
-        hops = lambda q, d: n // 2 - (0 if (d == 1) == (q % 2 == 0) else 1)
-        for h in range(n // 2):
-            for q in order:
-                if h == 0 and q:
-                    firsts[q - 1].wait_recv()
-                for d in (1, -1):
-                    if h >= hops(q, d):
-                        continue
-                    if h:
-                        copies[q, d, h - 1].wait_recv()
-                    part_of, k = piece(q, -d * h), len(copies)
-                    copies[q, d, h] = send(part_of, part_of, bs.at[k], br.at[k], toward[d])
+    def piece(core, x, z):
+        rows, at = rows_of(kept_rows(core, x, z), 16), pl.ds(al(kept_cols(core, x, z), 128), 640)
+        return gather.at[:, rows, at]
+
+    def z_off(i):
+        return (me.z + i + NZ) % NZ
+
+    def x_off(i):
+        return (me.x + i + NX) % NX
+
+    def put(copies, key, src, who):
+        k = len(copies)
+        copies[key] = send(src, src, bs.at[k], br.at[k], who)
+
+    @pl.when(me.c == 0)
+    def _():
+        mine = piece(0, me.x, me.z)
+        firsts = {i: send(mine, mine, as_.at[i - 1], ar.at[i - 1], me.peer(x=i)) for i in (2, 1, 3)}
+        copies, order = {}, (0, 1, 3, 2)
+        for q in order:
+            if q:
+                firsts[q].wait_recv()
+            for away in (2, -2, 1, -1):
+                put(copies, (q, away), piece(0, x_off(-q), me.z), me.peer(z=away))
         for q in order:
             for d in (1, -1):
-                copies[q, d, hops(q, d) - 1].wait_recv()
-        for copy in firsts + list(copies.values()):
+                copies[q, 2 * d].wait_recv()
+                came = piece(0, x_off(-q), z_off(-2 * d))
+                if (q in (0, 3)) == (d == 1):
+                    put(copies, (q, 4), came, me.peer(z=2 * d))
+                put(copies, (q, 3 * d), came, me.peer(z=d))
+        for q in order:
+            for key in (1, -1, 3, -3, 4):
+                copies[q, key].wait_recv()
+        for copy in list(firsts.values()) + list(copies.values()):
             copy.wait_send()
-
-    def owned(row, at):
-        return gather.at[:, rows_of(row + 16 * (at // 2), 16), pl.ds(al((at % 2) * 640, 128), 640)]
-
-    @pl.when(me.c == 0)
-    def _():
-        piece = lambda q, far: owned(32 * ((me.z + far + NZ) % NZ), (me.x - q + NX) % NX)
-        gather_all(X_PEERS, (0, 1, 3, 2), NZ, piece, me.peer(z=1), me.peer(z=-1))
 
     @pl.when(me.c == 1)
     def _():
-        piece = lambda q, far: owned(64 * ((me.x + far + NX) % NX), (me.z - q + NZ) % NZ)
-        gather_all(Z_PEERS, (0, 1, 7, 2, 6, 3, 5, 4), NX, piece, me.peer(x=1), me.peer(x=-1))
+        copies, xcopies = {}, {}
+        mine = piece(1, me.x, me.z)
+
+        def along_x(dz):
+            at = piece(1, me.x, z_off(dz))
+            for d in (1, -1):
+                put(xcopies, (dz, d), at, me.peer(x=d))
+
+        firsts = {}
+        for i, away in enumerate((2, -2, 1, -1)):
+            firsts[away] = send(mine, mine, as_.at[i], ar.at[i], me.peer(z=away))
+        along_x(0)
+        for d in (1, -1):
+            firsts[2 * d].wait_recv()
+            came = piece(1, me.x, z_off(-2 * d))
+            half = came.at[pl.ds(0 if d == 1 else 2, 2)]
+            k = 4 if d == 1 else 6
+            firsts[4 * d] = send(half, half, as_.at[k], ar.at[k], me.peer(z=2 * d))
+            firsts[3 * d] = send(came, came, as_.at[k + 1], ar.at[k + 1], me.peer(z=d))
+        for d in (1, -1):
+            firsts[d].wait_recv()
+            along_x(-d)
+        for d in (1, -1):
+            along_x(-2 * d)
+        for d in (1, -1):
+            firsts[3 * d].wait_recv()
+            along_x(-3 * d)
+        for d in (1, -1):
+            firsts[4 * d].wait_recv()
+        along_x(-4)
+        for dz in (0, -1, 1, -2, 2, -3, 3, -4):
+            d = 1 if dz % 2 == 0 else -1
+            xcopies[dz, d].wait_recv()
+            put(xcopies, (dz, 2), piece(1, x_off(-d), z_off(dz)), me.peer(x=d))
+        for dz in (0, -1, 1, -2, 2, -3, 3, -4):
+            d = 1 if dz % 2 == 0 else -1
+            xcopies[dz, -d].wait_recv()
+            xcopies[dz, 2].wait_recv()
+        for copy in list(firsts.values()) + list(xcopies.values()):
+            copy.wait_send()
 
     outs = []
     for s in range(4):
@@ -459,9 +577,9 @@
     xring.finish()
     to_mate.wait_send()
     to_mate_part.wait_send()
-    for copy in later + exchanged + crossed + stats + tables + list(hidden.values()) + [grads[i] for i in range(6)]:
+    for copy in later + id_copies + exchanged + crossed + stats + tables + list(hidden.values()) + [grads[i] for i in range(6)]:
         copy.wait_send()
-    for copy in outs:
+    for copy in outs + [gw_out]:
         copy.wait()
 
 
@@ -480,20 +598,20 @@
             jax.ShapeDtypeStruct((WIDE, VOCAB), BF16),
         ),
         in_specs=[hbm, hbm, vmem, vmem, vmem, vmem, smem],
-        out_specs=(vmem, hbm, vmem),
+        out_specs=(vmem, hbm, hbm),
         scratch_shapes=[
-            buf(WIDE, VOCAB), buf(ALL, WIDE), wide(OWN, VOCAB), wide(OWN, VOCAB), wide(OWN, VOCAB),
+            buf(WIDE, VOCAB), buf(VOCAB, WIDE), buf(ALL, WIDE), wide(OWN, VOCAB), wide(OWN, VOCAB), wide(OWN, VOCAB),
             wide(STEPS, STEP, VOCAB), wide(STEPS, STEP, VOCAB), wide(STEPS, STEP, VOCAB), wide(STEPS, STEP, VOCAB),
-            wide(16, VOCAB), wide(OWN, 128), wide(OWN, 128), wide(OWN, 128), wide(2, 8, OWN), wide(14, 8, OWN),
-            wide(4, 8, OWN), wide(OWN, 128),
-            buf(OWN, VOCAB), buf(ALL, VOCAB), wide(4, OWN, WIDE),
+            wide(16, VOCAB), pltpu.VMEM((4, 16, 16), jnp.int32), wide(ALL, 128), wide(OWN, 128), wide(OWN, 128), wide(2, 8, OWN), wide(14, 8, OWN),
+            wide(4, 8, OWN), wide(ALL, 128),
+            buf(OWN, VOCAB), buf(ALL, VOCAB), wide(4, OWN, WIDE), wide(ALL, WIDE), buf(WIDE, VOCAB),
             buf(28, 16, 1280), buf(28, 16, 1280), buf(12, 32, 1280), buf(12, 32, 1280),
             buf(2, 32, 1280), buf(2, 64, 1280), buf(3, 2, 16, 640), buf(7, 2, 16, 640), buf(2, 2, 16, 640),
             buf(7, 16, 640), buf(4, OWN, WIDE),
-            dma(6), dma(16), dma(16), dma(1), dma(1), dma(1), dma(1), dma(8), dma(8), dma(8), dma(8),
+            dma(7), dma(3), dma(3), dma(16), dma(16), dma(1), dma(1), dma(1), dma(1), dma(8), dma(8), dma(8), dma(8),
             dma(14), dma(14), dma(10), dma(10), dma(3), dma(3),
             dma(28), dma(28), dma(12), dma(12), dma(3), dma(3), dma(7), dma(7), dma(7), dma(7),
-            dma(7), dma(7), dma(28), dma(28),
+            dma(8), dma(8), dma(28), dma(28),
         ],
         compiler_params=pltpu.CompilerParams(
             collective_id=0, has_side_effects=True, vmem_limit_bytes=56 << 20

time: 142 us -> 139 us (0.979)
  Pallas kernels: 135 us -> 130 us
    pallas_call x1, Pallas kernels: 135 us -> 130 us  [fused(): pl.pallas_call(kernel, out_shape=(jax.ShapeDtypeStruct((16, 16), F32), ja...]
where the time goes in v5:
time: 139 us; the launch traced here: 138 us
  Pallas kernels  130 us (94%)
  local copies, waits for them, and re-layouts  6.56 us (5%)
    pallas_call x1, Pallas kernels, fused(): pl.pallas_call(kernel, out_shape=(jax.ShapeDtypeStruct((16, 16), F32), ja...  130 us
    unnamed x5, local copies, waits for them, and re-layouts  6.56 us

profile of v5, /device:TPU:32, one launch (start us, length us, event | category | flops | bytes accessed | tf_op | source)
XLA Modules:
  0.0 137.6 jit_solution(4867262840519891294)
XLA Ops:
  0.6 130.4 %fused.1 = (f32[16,16]{1,0:T(8,128)}, bf16[256,5120]{1,0:T(8,128)(2,1)}, bf16[1280,1280]{1,0:T(8,128)(2,1)}) custom-call(bf16[256,5120]{1,0:T(8,128)(2,1)} %hid_ref.1, bf16[1280,1280]{1,0:T(8,128)(2,1)} %w_hbm.1, s32[16,32]{1,0:T(8,128)} %pid_ref.1, s32[16,32]{1,0:T(8,128)} %pc_ref.1, s32[16,16]{1,0:T(8,128)} %sid_ref.1, s32[16,16]{1,0:T(8,128)} %mask_ref.1, ...), custom_call_target="tpu_custom_call" | custom-call | tf_op jit(solution)/shard_map/fused/pallas_call | solution.py:593
  131.0 0.0 copy-start
  131.0 1.4 %copy.13 = f32[16,16]{1,0:T(8,128)} copy(f32[16,16]{1,0:T(8,128)} %get-tuple-element.6) | data formatting | bytes 2048
  132.5 3.4 %copy.14 = bf16[256,5120]{1,0:T(8,128)(2,1)} copy(bf16[256,5120]{1,0:T(8,128)(2,1)} %get-tuple-element.7) | data formatting | bytes 5242880
  135.9 0.0 copy-done
  135.9 1.7 %copy.15 = bf16[1280,1280]{1,0:T(8,128)(2,1)} copy(bf16[1280,1280]{1,0:T(8,128)(2,1)S(1)} %copy-done) | data formatting | bytes 6553600
Async XLA Ops:
  131.0 4.9 %copy-start = (bf16[1280,1280]{1,0:T(8,128)(2,1)S(1)}, bf16[1280,1280]{1,0:T(8,128)(2,1)}, u32[]{:S(2)}) copy-start(bf16[1280,1280]{1,0:T(8,128)(2,1)} %get-tuple-element.8) | copy-start | bytes 9830404

commit v6 on v5

--- a/solution.py
+++ b/solution.py
@@ -207,21 +207,15 @@
     copy_h.wait()
     to_mate.wait_recv()
 
-    @pl.loop(0, 4)
-    def _(i):
-        at = rows_of(mates * OWN + i * 64, 64)
-        pout[rows_of(i * 64, 64)] = jnp.dot(hd[at, :], w_ref[...], preferred_element_type=F32)
-
+    pout[...] = jnp.dot(hd[rows_of(mates * OWN, OWN), :], w_ref[...], preferred_element_type=F32)
     to_mate_part = send(pout, pland, ps.at[0], pr.at[0], mate)
     exchanged, crossed = [], []
     vocab = (lax.broadcasted_iota(jnp.int32, (STEP, VOCAB), 1) + offset).astype(F32)
-    vocab_wide = (lax.broadcasted_iota(jnp.int32, (64, VOCAB), 1) + offset).astype(F32)
+    vocab_wide = (lax.broadcasted_iota(jnp.int32, (OWN, VOCAB), 1) + offset).astype(F32)
 
     def sampled_rows(j):
-        @pl.loop(0, 4)
-        def _(i):
-            chosen = jnp.where(vocab_wide == id_ref[rows_of(j * OWN + i * 64, 64), 0:1], 1.0, 0.0)
-            part[j, rows_of(i * 64, 64)] = jnp.dot(chosen.astype(BF16), wt_ref[...], preferred_element_type=F32)
+        chosen = jnp.where(vocab_wide == id_ref[rows_of(j * OWN, OWN), 0:1], 1.0, 0.0).astype(BF16)
+        part[j] = jnp.dot(chosen, wt_ref[...], preferred_element_type=F32)
 
     for s in range(STEPS):
         for rel in range(2):
@@ -237,17 +231,8 @@
             if i < len(wrapped):
                 for rel in range(2):
                     hidden[rel, wrapped[i]].start()
-        exchanged[s].wait_recv()
-        lout[s] = term[STEP:] + xland[s]
-        crossed.append(send(lout.at[s], lland.at[s], ls.at[s], lr.at[s], across))
         if s == 1:
-
-            @pl.loop(0, 4)
-            def _(i):
-                lex[rows_of(i * 64, 64)] = jnp.dot(
-                    hd[rows_of(own * OWN + i * 64, 64), :], w_ref[...], preferred_element_type=F32
-                )
-
+            lex[...] = jnp.dot(hd[rows_of(own * OWN, OWN), :], w_ref[...], preferred_element_type=F32)
         if s == 2:
             for copy in id_copies:
                 copy.wait_recv()
@@ -256,6 +241,9 @@
                 id_ref[rows_of(j * OWN, OWN)] = as_column(sids[j].astype(F32))
         if 3 <= s < 7:
             sampled_rows(s - 3)
+        exchanged[s].wait_recv()
+        lout[s] = term[STEP:] + xland[s]
+        crossed.append(send(lout.at[s], lland.at[s], ls.at[s], lr.at[s], across))
 
     grads = {}
 

time: 139 us -> 135 us (0.971)
  Pallas kernels: 130 us -> 126 us
    pallas_call x1, Pallas kernels: 130 us -> 126 us  [fused(): pl.pallas_call(kernel, out_shape=(jax.ShapeDtypeStruct((16, 16), F32), ja...]
where the time goes in v6:
time: 135 us; the launch traced here: 133 us
  Pallas kernels  126 us (93%)
  local copies, waits for them, and re-layouts  6.56 us (5%)
    pallas_call x1, Pallas kernels, fused(): pl.pallas_call(kernel, out_shape=(jax.ShapeDtypeStruct((16, 16), F32), ja...  126 us
    unnamed x5, local copies, waits for them, and re-layouts  6.56 us

profile of v6, /device:TPU:32, one launch (start us, length us, event | category | flops | bytes accessed | tf_op | source)
XLA Modules:
  0.0 133.5 jit_solution(12773867449450730750)
XLA Ops:
  0.6 126.3 %fused.1 = (f32[16,16]{1,0:T(8,128)}, bf16[256,5120]{1,0:T(8,128)(2,1)}, bf16[1280,1280]{1,0:T(8,128)(2,1)}) custom-call(bf16[256,5120]{1,0:T(8,128)(2,1)} %hid_ref.1, bf16[1280,1280]{1,0:T(8,128)(2,1)} %w_hbm.1, s32[16,32]{1,0:T(8,128)} %pid_ref.1, s32[16,32]{1,0:T(8,128)} %pc_ref.1, s32[16,16]{1,0:T(8,128)} %sid_ref.1, s32[16,16]{1,0:T(8,128)} %mask_ref.1, ...), custom_call_target="tpu_custom_call" | custom-call | tf_op jit(solution)/shard_map/fused/pallas_call | solution.py:581
  126.9 0.0 copy-start
  126.9 1.4 %copy.13 = f32[16,16]{1,0:T(8,128)} copy(f32[16,16]{1,0:T(8,128)} %get-tuple-element.6) | data formatting | bytes 2048
  128.4 3.4 %copy.14 = bf16[256,5120]{1,0:T(8,128)(2,1)} copy(bf16[256,5120]{1,0:T(8,128)(2,1)} %get-tuple-element.7) | data formatting | bytes 5242880
  131.8 0.0 copy-done
  131.8 1.7 %copy.15 = bf16[1280,1280]{1,0:T(8,128)(2,1)} copy(bf16[1280,1280]{1,0:T(8,128)(2,1)S(1)} %copy-done) | data formatting | bytes 6553600
Async XLA Ops:
  126.9 4.9 %copy-start = (bf16[1280,1280]{1,0:T(8,128)(2,1)S(1)}, bf16[1280,1280]{1,0:T(8,128)(2,1)}, u32[]{:S(2)}) copy-start(bf16[1280,1280]{1,0:T(8,128)(2,1)} %get-tuple-element.8) | copy-start | bytes 9830404

commit v7 on v6

--- a/solution.py
+++ b/solution.py
@@ -182,7 +182,7 @@
     for s in range(STEPS):
         for rel in range(2):
             hidden[rel, s] = hidden_copy(rel, s, toward if s in DIRECT else -toward)
-    ahead = 2
+    ahead = 3
     for s in (wrapped[0],) + DIRECT[:1]:
         for rel in range(2):
             hidden[rel, s].start()
@@ -217,6 +217,7 @@
         chosen = jnp.where(vocab_wide == id_ref[rows_of(j * OWN, OWN), 0:1], 1.0, 0.0).astype(BF16)
         part[j] = jnp.dot(chosen, wt_ref[...], preferred_element_type=F32)
 
+    sampled_rows(own)
     for s in range(STEPS):
         for rel in range(2):
             hidden[rel, s].wait_recv()
@@ -239,8 +240,8 @@
             for i in range(1, 4):
                 j = (own + i) % 4
                 id_ref[rows_of(j * OWN, OWN)] = as_column(sids[j].astype(F32))
-        if 3 <= s < 7:
-            sampled_rows(s - 3)
+        if 3 <= s < 6:
+            sampled_rows((own + s - 2) % 4)
         exchanged[s].wait_recv()
         lout[s] = term[STEP:] + xland[s]
         crossed.append(send(lout.at[s], lland.at[s], ls.at[s], lr.at[s], across))
@@ -422,10 +423,9 @@
             send(cut(x2, (me.z + i) % NZ), x2land.at[i - 1], x2s.at[i - 1], x2r.at[i - 1], me.peer(z=i))
         )
     zring.step(LATE, 0, 3)
-    turn(0, 16)
+    turn(0, 8)
     zring.step(LATE, 1, 3)
-    turn(16, 32)
-    weight_tiles(0, 2)
+    turn(8, 16)
     for half, ylo in ((EARLY, me.ylo), (LATE, 1 - me.ylo)):
         for sub in range(2):
             z2[ylo, pl.ds(sub * 16, 16)] = zring.total(half, sub).astype(BF16)
@@ -434,7 +434,7 @@
         z_copies.append(
             send(cut(z2, (me.x + i) % NX), z2land.at[i - 1], z2s.at[i - 1], z2r.at[i - 1], me.peer(x=i))
         )
-    weight_tiles(2, 6)
+    turn(16, 32)
     for core, (ours, land, copies) in enumerate(
         ((cut(z2, me.x), z2land, z_copies), (cut(x2, me.z), x2land, x_copies))
     ):
@@ -456,9 +456,8 @@
     for i, s in enumerate(Y_PEERS):
         piece = ysum.at[(me.c + s["c"]) % 2, (me.ylo + s["y"]) % 2]
         y_copies[s["y"], s["c"]] = send(piece, yland.at[i], ys.at[i], yr.at[i], me.peer(**s))
-    weight_tiles(6, 10)
+    weight_tiles(0, 3)
     gw_out = pltpu.make_async_copy(gw_tiles, gw_ref, loc.at[6])
-    gw_out.start()
     row, col = kept_rows(0, me.x, me.z), kept_cols(0, me.x, me.z)
     row = jnp.where(me.c == 0, row, kept_rows(1, me.x, me.z))
     col = jnp.where(me.c == 0, col, kept_cols(1, me.x, me.z))
@@ -495,21 +494,25 @@
         mine = piece(0, me.x, me.z)
         firsts = {i: send(mine, mine, as_.at[i - 1], ar.at[i - 1], me.peer(x=i)) for i in (2, 1, 3)}
         copies, order = {}, (0, 1, 3, 2)
-        for q in order:
-            if q:
-                firsts[q].wait_recv()
-            for away in (2, -2, 1, -1):
-                put(copies, (q, away), piece(0, x_off(-q), me.z), me.peer(z=away))
+        hops = lambda q, d: NZ // 2 - (0 if (d == 1) == (q in (0, 3)) else 1)
+        for h in range(NZ // 2):
+            for q in order:
+                if h == 0 and q:
+                    firsts[q].wait_recv()
+                for d in (1, -1):
+                    if h >= hops(q, d):
+                        continue
+                    if h:
+                        copies[q, d, h - 1].wait_recv()
+                    put(copies, (q, d, h), piece(0, x_off(-q), z_off(-d * h)), me.peer(z=d))
+                if h == 0 and q == 0:
+                    weight_tiles(3, 7)
+            if h == 0:
+                weight_tiles(7, 10)
+                gw_out.start()
         for q in order:
             for d in (1, -1):
-                copies[q, 2 * d].wait_recv()
-                came = piece(0, x_off(-q), z_off(-2 * d))
-                if (q in (0, 3)) == (d == 1):
-                    put(copies, (q, 4), came, me.peer(z=2 * d))
-                put(copies, (q, 3 * d), came, me.peer(z=d))
-        for q in order:
-            for key in (1, -1, 3, -3, 4):
-                copies[q, key].wait_recv()
+                copies[q, d, hops(q, d) - 1].wait_recv()
         for copy in list(firsts.values()) + list(copies.values()):
             copy.wait_send()
 
@@ -527,6 +530,7 @@
         for i, away in enumerate((2, -2, 1, -1)):
             firsts[away] = send(mine, mine, as_.at[i], ar.at[i], me.peer(z=away))
         along_x(0)
+        weight_tiles(3, 7)
         for d in (1, -1):
             firsts[2 * d].wait_recv()
             came = piece(1, me.x, z_off(-2 * d))
@@ -542,6 +546,8 @@
         for d in (1, -1):
             firsts[3 * d].wait_recv()
             along_x(-3 * d)
+        weight_tiles(7, 10)
+        gw_out.start()
         for d in (1, -1):
             firsts[4 * d].wait_recv()
         along_x(-4)

time: 135 us -> 132 us (0.978); the launches traced: 133 us -> 132 us
    pallas_call x1, Pallas kernels: 126 us -> 125 us  [fused(): pl.pallas_call(kernel, out_shape=(jax.ShapeDtypeStruct((16, 16), F32), ja...]
where the time goes in v7:
time: 132 us
  Pallas kernels  125 us (95%)
  local copies, waits for them, and re-layouts  6.56 us (5%)
    pallas_call x1, Pallas kernels, fused(): pl.pallas_call(kernel, out_shape=(jax.ShapeDtypeStruct((16, 16), F32), ja...  125 us
    unnamed x5, local copies, waits for them, and re-layouts  6.56 us

profile of v7, /device:TPU:32, one launch (start us, length us, event | category | flops | bytes accessed | tf_op | source)
XLA Modules:
  0.0 132.0 jit_solution(10994680246574228752)
XLA Ops:
  0.6 124.8 %fused.1 = (f32[16,16]{1,0:T(8,128)}, bf16[256,5120]{1,0:T(8,128)(2,1)}, bf16[1280,1280]{1,0:T(8,128)(2,1)}) custom-call(bf16[256,5120]{1,0:T(8,128)(2,1)} %hid_ref.1, bf16[1280,1280]{1,0:T(8,128)(2,1)} %w_hbm.1, s32[16,32]{1,0:T(8,128)} %pid_ref.1, s32[16,32]{1,0:T(8,128)} %pc_ref.1, s32[16,16]{1,0:T(8,128)} %sid_ref.1, s32[16,16]{1,0:T(8,128)} %mask_ref.1, ...), custom_call_target="tpu_custom_call" | custom-call | tf_op jit(solution)/shard_map/fused/pallas_call | solution.py:587
  125.4 0.0 copy-start
  125.4 1.4 %copy.13 = f32[16,16]{1,0:T(8,128)} copy(f32[16,16]{1,0:T(8,128)} %get-tuple-element.6) | data formatting | bytes 2048
  126.9 3.4 %copy.14 = bf16[256,5120]{1,0:T(8,128)(2,1)} copy(bf16[256,5120]{1,0:T(8,128)(2,1)} %get-tuple-element.7) | data formatting | bytes 5242880
  130.3 0.0 copy-done
  130.3 1.7 %copy.15 = bf16[1280,1280]{1,0:T(8,128)(2,1)} copy(bf16[1280,1280]{1,0:T(8,128)(2,1)S(1)} %copy-done) | data formatting | bytes 6553600
Async XLA Ops:
  125.4 4.9 %copy-start = (bf16[1280,1280]{1,0:T(8,128)(2,1)S(1)}, bf16[1280,1280]{1,0:T(8,128)(2,1)}, u32[]{:S(2)}) copy-start(bf16[1280,1280]{1,0:T(8,128)(2,1)} %get-tuple-element.8) | copy-start | bytes 9830404

commit v8 on v7

--- a/solution.py
+++ b/solution.py
@@ -376,10 +376,10 @@
     scale(mates, 0)
     scale(mates, 1)
     begin(EARLY, 0)
+    relay(2)
     begin(EARLY, 1)
+    relay(3)
     late(0)
-    relay(2)
-    relay(3)
     product(mine_of, PART, PART, gr, mine_of * OWN)
     zring.step(EARLY, 0, 1)
     xring.step(EARLY, 0, 1)

time: 132 us -> 132 us (level)
  no operation moved by 1% of the time
where the time goes in v8:
time: 132 us
  Pallas kernels  125 us (95%)
  local copies, waits for them, and re-layouts  6.56 us (5%)
    pallas_call x1, Pallas kernels, fused(): pl.pallas_call(kernel, out_shape=(jax.ShapeDtypeStruct((16, 16), F32), ja...  125 us
    unnamed x5, local copies, waits for them, and re-layouts  6.56 us

profile of v8, /device:TPU:32, one launch (start us, length us, event | category | flops | bytes accessed | tf_op | source)
XLA Modules:
  0.0 131.9 jit_solution(14623589329698568237)
XLA Ops:
  0.6 124.7 %fused.1 = (f32[16,16]{1,0:T(8,128)}, bf16[256,5120]{1,0:T(8,128)(2,1)}, bf16[1280,1280]{1,0:T(8,128)(2,1)}) custom-call(bf16[256,5120]{1,0:T(8,128)(2,1)} %hid_ref.1, bf16[1280,1280]{1,0:T(8,128)(2,1)} %w_hbm.1, s32[16,32]{1,0:T(8,128)} %pid_ref.1, s32[16,32]{1,0:T(8,128)} %pc_ref.1, s32[16,16]{1,0:T(8,128)} %sid_ref.1, s32[16,16]{1,0:T(8,128)} %mask_ref.1, ...), custom_call_target="tpu_custom_call" | custom-call | tf_op jit(solution)/shard_map/fused/pallas_call | solution.py:587
  125.4 0.0 copy-start
  125.4 1.4 %copy.13 = f32[16,16]{1,0:T(8,128)} copy(f32[16,16]{1,0:T(8,128)} %get-tuple-element.6) | data formatting | bytes 2048
  126.8 3.4 %copy.14 = bf16[256,5120]{1,0:T(8,128)(2,1)} copy(bf16[256,5120]{1,0:T(8,128)(2,1)} %get-tuple-element.7) | data formatting | bytes 5242880
  130.2 0.0 copy-done
  130.2 1.7 %copy.15 = bf16[1280,1280]{1,0:T(8,128)(2,1)} copy(bf16[1280,1280]{1,0:T(8,128)(2,1)S(1)} %copy-done) | data formatting | bytes 6553600
Async XLA Ops:
  125.4 4.9 %copy-start = (bf16[1280,1280]{1,0:T(8,128)(2,1)S(1)}, bf16[1280,1280]{1,0:T(8,128)(2,1)}, u32[]{:S(2)}) copy-start(bf16[1280,1280]{1,0:T(8,128)(2,1)} %get-tuple-element.8) | copy-start | bytes 9830404
